TPU v7x, 512 devices: a whole 4x8x8 slice. The times are simulated.
512 devices in a mesh: tm: 32 (over y_hi, z), space: 16 (over y_lo, x, core).
Axes of the slice: x: 4, y: 8 (y_hi: 4, y_lo: 2; y = y_hi * 2 + y_lo), z: 8, core: 2. Of those that a mesh axis runs over, the one named last changes fastest.
Arguments:
- previous: float32 [64, 3, 512, 512], P('tm', None, 'space'), may hold values from -6 to 6
- right_side: float32 [64, 3, 512, 512], P('tm', None, 'space'), may hold values from -6 to 6
- kappa: float32 [3, 512, 512], P(None, 'space'), may hold values from 0.2 to 2
- drift: float32 [3, 2], replicated, may hold values from -0.4 to 0.4
- reaction: float32 [3, 3], replicated, may hold values from -0.3 to 1.2, as said below
Outputs:
- new_iterate: float32 [64, 3, 512, 512], P('tm', None, 'space')
- residual: float32 [64, 3, 512, 512], P('tm', None, 'space')
Inputs may be any that keep to these rules, and one draw needn't show every extreme that they name: `reaction`: off the diagonal in -0.3 to 0.3, on it 0.6 to 1.2.
All inputs are finite; a program needn't handle non-finite values.
Results may differ from a plain program's by a relative error of at most 0.0003.
Values sent between devices are 32-bit elements; how exact they have to be, the bound alone decides.
A program may use at most 64 MiB of HBM per device.

v0:
```python
import math

import jax
import jax.numpy as jnp
from jax import lax
from jax.sharding import PartitionSpec as P

STEPS = 64
SWEEPS = 6


ALPHA = 0.2
highest = lax.Precision.HIGHEST


def spread(shard, axis, root):
    mine = lax.axis_index(axis) == root
    return lax.psum(jnp.where(mine, shard, jnp.zeros_like(shard)), axis)


def padded_2(shard, sides, width):
    for axis, dim in sides:
        count, length = (lax.axis_size(axis), shard.shape[dim])
        up = [(i, (i + 1) % count) for i in range(count - 1)]
        down = [(j, i) for i, j in up]
        last = lax.slice_in_dim(shard, length - width, length, axis=dim)
        leading = lax.slice_in_dim(shard, 0, width, axis=dim)
        before = lax.ppermute(last, axis, up)
        after = lax.ppermute(leading, axis, down)
        shard = jnp.concatenate([before, shard, after], axis=dim)
    return shard


def from_behind(shard, axis, by):
    count = lax.axis_size(axis)
    pairs = [(i, i + by) for i in range(count) if 0 <= i + by < count]
    return lax.ppermute(shard, axis, pairs)


def time_tables():
    counts = jnp.arange(STEPS, dtype=jnp.int32)
    product = counts[:, None] * counts[None, :] % STEPS
    angles = product.astype(jnp.float32) * (2.0 * math.pi / STEPS)
    weights = jnp.power(ALPHA, counts.astype(jnp.float32) / STEPS)
    forward_cos = jnp.cos(angles) * weights[None, :] / STEPS
    forward_sin = jnp.sin(angles) * weights[None, :] / STEPS
    inverse_cos = jnp.cos(angles) / weights[:, None]
    inverse_sin = jnp.sin(angles) / weights[:, None]
    rooted = ALPHA ** (1.0 / STEPS)
    phases = counts.astype(jnp.float32) * (2.0 * math.pi / STEPS)
    eigen_re = 1.0 - rooted * jnp.cos(phases)
    eigen_im = -rooted * jnp.sin(phases)
    return (forward_cos, forward_sin, inverse_cos, inverse_sin, eigen_re, eigen_im)


def cross_terms(center, upper, lower, plus_y, minus_y, kappa, drift, react_off):
    drift_x = drift[:, 0][:, None, None]
    drift_y = drift[:, 1][:, None, None]
    mixing = jnp.einsum("cd,...dxy->...cxy", react_off, center, precision=highest)
    return (
        0.5 * drift_x * (upper - lower)
        + 0.5 * drift_y * (plus_y - minus_y)
        - kappa * (upper + lower + plus_y + minus_y)
        + mixing
    )


def neighbour_terms(center, upper, lower, kappa, drift, react_off):
    plus_y = jnp.roll(center, -1, -1)
    minus_y = jnp.roll(center, 1, -1)
    return cross_terms(center, upper, lower, plus_y, minus_y, kappa, drift, react_off)


def shards(previous, right_side, kappa, drift, reaction):
    local_steps, fields, rows, width = previous.shape
    tm_count = lax.axis_size("tm")
    freq_count = STEPS // tm_count
    forward_cos, forward_sin, inverse_cos, inverse_sin, eigen_re, eigen_im = time_tables()
    identity = jnp.eye(fields, dtype=jnp.float32)
    react_off = reaction * (1.0 - identity)
    react_diag = jnp.diagonal(reaction)[:, None, None]
    carried = spread(previous[local_steps - 1], "tm", tm_count - 1)
    wrap_term = -ALPHA / STEPS * carried

    def sweep(resid, inv_re, inv_im):
        return jnp.stack(
            [resid[0] * inv_re - resid[1] * inv_im, resid[0] * inv_im + resid[1] * inv_re]
        )

    blocks = right_side.reshape(local_steps, fields * rows, width)
    gathered = lax.all_to_all(blocks, "tm", split_axis=1, concat_axis=0, tiled=True)
    spectrum = lax.all_to_all(
        jnp.stack(
            [
                jnp.einsum("kn,npy->kpy", forward_cos, gathered, precision=highest),
                jnp.einsum("kn,npy->kpy", forward_sin, gathered, precision=highest),
            ]
        ),
        "tm",
        split_axis=1,
        concat_axis=2,
        tiled=True,
    )
    spectrum = spectrum.reshape(2, freq_count, fields, rows, width)
    spectrum = spectrum.at[0].add(wrap_term[None])
    first_freq = lax.axis_index("tm") * freq_count
    lam_re = lax.dynamic_slice_in_dim(eigen_re, first_freq, freq_count)[:, None, None, None]
    lam_im = lax.dynamic_slice_in_dim(eigen_im, first_freq, freq_count)[:, None, None, None]
    diag_re = lam_re + (4.0 * kappa + react_diag)
    diag_im = lam_im + jnp.zeros_like(kappa)
    magnitude = diag_re * diag_re + diag_im * diag_im
    inv_re = diag_re / magnitude
    inv_im = -diag_im / magnitude
    solution = sweep(spectrum, inv_re, inv_im)
    for repeat in range(SWEEPS - 1):
        padded = padded_2(solution, (("space", 3),), 1)
        off = neighbour_terms(
            solution, padded[:, :, :, 2:, :], padded[:, :, :, :-2, :], kappa, drift, react_off
        )
        solution = sweep(spectrum - off, inv_re, inv_im)
    stacked = solution.reshape(2, freq_count, fields * rows, width)
    gathered_back = lax.all_to_all(stacked, "tm", split_axis=2, concat_axis=1, tiled=True)
    physical = jnp.einsum(
        "nk,kpy->npy", inverse_cos, gathered_back[0], precision=highest
    ) + jnp.einsum("nk,kpy->npy", inverse_sin, gathered_back[1], precision=highest)
    new_iterate = lax.all_to_all(physical, "tm", split_axis=0, concat_axis=1, tiled=True).reshape(
        local_steps, fields, rows, width
    )
    padded = padded_2(new_iterate, (("space", 2),), 1)
    operated = (4.0 * kappa + react_diag) * new_iterate + neighbour_terms(
        new_iterate, padded[:, :, 2:, :], padded[:, :, :-2, :], kappa, drift, react_off
    )
    earlier = from_behind(new_iterate[local_steps - 1], "tm", 1)
    before = jnp.concatenate([earlier[None], new_iterate[:-1]], 0)
    residual = right_side - (new_iterate + operated - before)
    return (new_iterate, residual)


def solution(mesh):
    in_specs = (
        P("tm", None, "space", None),
        P("tm", None, "space", None),
        P(None, "space", None),
        P(),
        P(),
    )
    out_specs = (P("tm", None, "space", None), P("tm", None, "space", None))
    return jax.shard_map(shards, mesh=mesh, in_specs=in_specs, out_specs=out_specs, check_vma=False)
```

profile of v0, /device:TPU:1, one launch (start us, length us, event | category | flops | bytes accessed | tf_op | source)
XLA Modules:
  0.0 494.8 jit_solution(11562252318456479654)
XLA Ops:
  7.2 2.0 copy.117
  9.2 16.5 %all-to-all-start = ((f32[2,96,512]{2,0,1:T(2,128)}), f32[2,96,512]{2,0,1:T(2,128)S(1)}, u32[]{:S(2)}, u32[]{:S(2)}) async-start(f32[2,96,512]{2,0,1:T(2,128)} %copy.117), calls=%async_computation | async-start | bytes 786432 | tf_op jit(solution)/shard_map/all_to_all | solution.py:91
  25.7 14.6 %all-to-all-done = f32[2,96,512]{2,0,1:T(2,128)S(1)} async-done(((f32[2,96,512]{2,0,1:T(2,128)}), f32[2,96,512]{2,0,1:T(2,128)S(1)}, u32[]{:S(2)}, u32[]{:S(2)}) %all-to-all-start) | async-done | bytes 393248 | tf_op jit(solution)/shard_map/all_to_all | solution.py:91
  43.5 7.5 %all-to-all-start.1 = ((f32[2,64,3,512]{3,0,2,1:T(2,128)}), f32[2,64,3,512]{3,0,2,1:T(2,128)S(1)}, u32[]{:S(2)}, u32[]{:S(2)}) async-start(f32[2,64,3,512]{3,0,2,1:T(2,128)} %copy.119), calls=%async_computation.1 | async-start | bytes 1572864 | tf_op jit(solution)/shard_map/all_to_all | solution.py:92
  54.0 285.0 %all-reduce.2.cloned.1.call-done = f32[3,32,512]{2,1,0:T(8,128)} async-done(((f32[3,32,512]{2,1,0:T(8,128)}), f32[3,32,512]{2,1,0:T(8,128)}) %all-reduce.2.cloned.1.call-update) | async-done | bytes 196624 | tf_op jit(solution)/shard_map/psum | solution.py:18
  341.4 22.0 %collective-permute-start = (f32[2,2,3,1,512]{4,3,2,1,0:T(1,128)S(1)}, f32[2,2,3,1,512]{4,3,2,1,0:T(1,128)S(1)}, u32[]{:S(2)}, u32[]{:S(2)}) collective-permute-start(f32[2,2,3,1,512]{4,3,2,1,0:T(1,128)S(1)} %get-tuple-element.63), channel_id=1, source_target_pairs={{1,0},{2,1},{3,2},{4,3},{5,4},{6,5},{7,6},{8,7},{9,8},{10,9},{11,1... | collective-permute-start | bytes 73736 | tf_op jit(solution)/shard_map/ppermute | solution.py:29
  363.4 2.2 collective-permute-start.1
  365.6 2.3 fusion.11
  369.5 2.2 collective-permute-start.2
  371.7 3.6 collective-permute-start.3
  375.3 2.3 fusion.9
  381.1 3.6 collective-permute-start.5
  384.8 2.3 fusion.7
  390.6 3.6 collective-permute-start.7
  394.3 2.3 fusion.5
  400.1 3.9 collective-permute-start.9
  404.0 2.3 fusion.3
  408.1 29.6 %all_to_all.63 = f32[2,2,96,512]{3,1,0,2:T(2,128)S(1)} all-to-all(f32[2,2,96,512]{3,1,0,2:T(2,128)S(1)} %copy.133), channel_id=1, replica_groups=mesh['tm'=32,'space'=16] {'tm'}, dimensions={2} | all-to-all | bytes 1572864 | tf_op jit(solution)/shard_map/all_to_all | solution.py:122
  441.2 10.5 %all-to-all-start.3 = ((f32[64,3,512]{2,1,0:T(4,128)}), f32[64,3,512]{2,1,0:T(4,128)S(1)}, u32[]{:S(2)}, u32[]{:S(2)}) async-start(f32[64,3,512]{2,1,0:T(4,128)} %copy.137), calls=%async_computation.3 | async-start | bytes 1048576 | tf_op jit(solution)/shard_map/all_to_all | solution.py:126
  452.0 14.5 %all-to-all-done.3 = f32[64,3,512]{2,1,0:T(4,128)S(1)} async-done(((f32[64,3,512]{2,1,0:T(4,128)}), f32[64,3,512]{2,1,0:T(4,128)S(1)}, u32[]{:S(2)}, u32[]{:S(2)}) %all-to-all-start.3) | async-done | bytes 393248 | tf_op jit(solution)/shard_map/all_to_all | solution.py:126
  468.5 4.6 collective-permute-start.12
  473.1 4.7 collective-permute-start.10
  477.8 5.4 %collective-permute-start.11 = (f32[2,3,1,512]{3,1,2,0:T(4,128)S(1)}, f32[2,3,1,512]{3,1,2,0:T(4,128)S(1)}, u32[]{:S(2)}, u32[]{:S(2)}) collective-permute-start(f32[2,3,1,512]{3,1,2,0:T(4,128)S(1)} %get-tuple-element.70), channel_id=1, source_target_pairs={{0,1},{1,2},{2,3},{3,4},{4,5},{5,6},{6,7},{7,8},{8,9},{9,10},{10,1... | collective-permute-start | bytes 36872 | tf_op jit(solution)/shard_map/ppermute | solution.py:28
  485.1 2.0 fusion.28
  (105 shorter events, 30.7 us)
Async XLA Ops:
  9.2 31.1 %all-to-all-start = ((f32[2,96,512]{2,0,1:T(2,128)}), f32[2,96,512]{2,0,1:T(2,128)S(1)}, u32[]{:S(2)}, u32[]{:S(2)}) async-start(f32[2,96,512]{2,0,1:T(2,128)} %copy.117), calls=%async_computation | async-start | bytes 786432 | tf_op jit(solution)/shard_map/all_to_all | solution.py:91
  43.5 7.6 %copy-start.3 = (f32[2,3,32,512]{3,2,1,0:T(8,128)S(1)}, f32[2,3,32,512]{3,2,1,0:T(8,128)}, u32[]{:S(2)}) copy-start(f32[2,3,32,512]{3,2,1,0:T(8,128)} %param.7) | copy-start | bytes 1179652
  43.5 296.5 %all-to-all-start.1 = ((f32[2,64,3,512]{3,0,2,1:T(2,128)}), f32[2,64,3,512]{3,0,2,1:T(2,128)S(1)}, u32[]{:S(2)}, u32[]{:S(2)}) async-start(f32[2,64,3,512]{3,0,2,1:T(2,128)} %copy.119), calls=%async_computation.1 | async-start | bytes 1572864 | tf_op jit(solution)/shard_map/all_to_all | solution.py:92
  51.0 288.0 %all-reduce.2.cloned.1.call-start = ((), (), s32[]{:S(2)}) async-start(), calls=%async_computation.4 | async-start | bytes 393216 | tf_op jit(solution)/shard_map/psum | solution.py:18
  51.8 0.7 copy-start
  52.5 286.6 %copy-start.1 = (f32[3,32,512]{2,1,0:T(8,128)S(1)}, f32[3,32,512]{2,1,0:T(8,128)}, u32[]{:S(2)}) copy-start(f32[3,32,512]{2,1,0:T(8,128)} %param.9) | copy-start | bytes 589828
  53.3 0.7 copy-start.4
  341.4 26.6 %collective-permute-start = (f32[2,2,3,1,512]{4,3,2,1,0:T(1,128)S(1)}, f32[2,2,3,1,512]{4,3,2,1,0:T(1,128)S(1)}, u32[]{:S(2)}, u32[]{:S(2)}) collective-permute-start(f32[2,2,3,1,512]{4,3,2,1,0:T(1,128)S(1)} %get-tuple-element.63), channel_id=1, source_target_pairs={{1,0},{2,1},{3,2},{4,3},{5,4},{6,5},{7,6},{8,7},{9,8},{10,9},{11,1... | collective-permute-start | bytes 73736 | tf_op jit(solution)/shard_map/ppermute | solution.py:29
  363.4 4.6 collective-permute-start.1
  369.5 8.2 %collective-permute-start.2 = (f32[2,2,3,1,512]{4,3,2,1,0:T(1,128)S(1)}, f32[2,2,3,1,512]{4,3,2,1,0:T(1,128)S(1)}, u32[]{:S(2)}, u32[]{:S(2)}) collective-permute-start(f32[2,2,3,1,512]{4,3,2,1,0:T(1,128)S(1)} %get-tuple-element.57), channel_id=1, source_target_pairs={{1,0},{2,1},{3,2},{4,3},{5,4},{6,5},{7,6},{8,7},{9,8},{10,9},{11,1... | collective-permute-start | bytes 73736 | tf_op jit(solution)/shard_map/ppermute | solution.py:29
  371.7 6.0 %collective-permute-start.3 = (f32[2,2,3,1,512]{4,3,2,1,0:T(1,128)S(1)}, f32[2,2,3,1,512]{4,3,2,1,0:T(1,128)S(1)}, u32[]{:S(2)}, u32[]{:S(2)}) collective-permute-start(f32[2,2,3,1,512]{4,3,2,1,0:T(1,128)S(1)} %get-tuple-element.56), channel_id=1, source_target_pairs={{0,1},{1,2},{2,3},{3,4},{4,5},{5,6},{6,7},{7,8},{8,9},{9,10},{10,1... | collective-permute-start | bytes 73736 | tf_op jit(solution)/shard_map/ppermute | solution.py:28
  379.2 8.0 %collective-permute-start.4 = (f32[2,2,3,1,512]{4,3,2,1,0:T(1,128)S(1)}, f32[2,2,3,1,512]{4,3,2,1,0:T(1,128)S(1)}, u32[]{:S(2)}, u32[]{:S(2)}) collective-permute-start(f32[2,2,3,1,512]{4,3,2,1,0:T(1,128)S(1)} %get-tuple-element.51), channel_id=1, source_target_pairs={{1,0},{2,1},{3,2},{4,3},{5,4},{6,5},{7,6},{8,7},{9,8},{10,9},{11,1... | collective-permute-start | bytes 73736 | tf_op jit(solution)/shard_map/ppermute | solution.py:29
  381.1 6.1 %collective-permute-start.5 = (f32[2,2,3,1,512]{4,3,2,1,0:T(1,128)S(1)}, f32[2,2,3,1,512]{4,3,2,1,0:T(1,128)S(1)}, u32[]{:S(2)}, u32[]{:S(2)}) collective-permute-start(f32[2,2,3,1,512]{4,3,2,1,0:T(1,128)S(1)} %get-tuple-element.50), channel_id=1, source_target_pairs={{0,1},{1,2},{2,3},{3,4},{4,5},{5,6},{6,7},{7,8},{8,9},{9,10},{10,1... | collective-permute-start | bytes 73736 | tf_op jit(solution)/shard_map/ppermute | solution.py:28
  388.7 8.0 %collective-permute-start.6 = (f32[2,2,3,1,512]{4,3,2,1,0:T(1,128)S(1)}, f32[2,2,3,1,512]{4,3,2,1,0:T(1,128)S(1)}, u32[]{:S(2)}, u32[]{:S(2)}) collective-permute-start(f32[2,2,3,1,512]{4,3,2,1,0:T(1,128)S(1)} %get-tuple-element.45), channel_id=1, source_target_pairs={{1,0},{2,1},{3,2},{4,3},{5,4},{6,5},{7,6},{8,7},{9,8},{10,9},{11,1... | collective-permute-start | bytes 73736 | tf_op jit(solution)/shard_map/ppermute | solution.py:29
  390.6 6.1 %collective-permute-start.7 = (f32[2,2,3,1,512]{4,3,2,1,0:T(1,128)S(1)}, f32[2,2,3,1,512]{4,3,2,1,0:T(1,128)S(1)}, u32[]{:S(2)}, u32[]{:S(2)}) collective-permute-start(f32[2,2,3,1,512]{4,3,2,1,0:T(1,128)S(1)} %get-tuple-element.44), channel_id=1, source_target_pairs={{0,1},{1,2},{2,3},{3,4},{4,5},{5,6},{6,7},{7,8},{8,9},{9,10},{10,1... | collective-permute-start | bytes 73736 | tf_op jit(solution)/shard_map/ppermute | solution.py:28
  398.2 8.2 %collective-permute-start.8 = (f32[2,2,3,1,512]{4,3,2,1,0:T(1,128)S(1)}, f32[2,2,3,1,512]{4,3,2,1,0:T(1,128)S(1)}, u32[]{:S(2)}, u32[]{:S(2)}) collective-permute-start(f32[2,2,3,1,512]{4,3,2,1,0:T(1,128)S(1)} %get-tuple-element.39), channel_id=1, source_target_pairs={{1,0},{2,1},{3,2},{4,3},{5,4},{6,5},{7,6},{8,7},{9,8},{10,9},{11,1... | collective-permute-start | bytes 73736 | tf_op jit(solution)/shard_map/ppermute | solution.py:29
  400.1 6.3 %collective-permute-start.9 = (f32[2,2,3,1,512]{4,3,2,1,0:T(1,128)S(1)}, f32[2,2,3,1,512]{4,3,2,1,0:T(1,128)S(1)}, u32[]{:S(2)}, u32[]{:S(2)}) collective-permute-start(f32[2,2,3,1,512]{4,3,2,1,0:T(1,128)S(1)} %get-tuple-element.38), channel_id=1, source_target_pairs={{0,1},{1,2},{2,3},{3,4},{4,5},{5,6},{6,7},{7,8},{8,9},{9,10},{10,1... | collective-permute-start | bytes 73736 | tf_op jit(solution)/shard_map/ppermute | solution.py:28
  441.2 25.3 %all-to-all-start.3 = ((f32[64,3,512]{2,1,0:T(4,128)}), f32[64,3,512]{2,1,0:T(4,128)S(1)}, u32[]{:S(2)}, u32[]{:S(2)}) async-start(f32[64,3,512]{2,1,0:T(4,128)} %copy.137), calls=%async_computation.3 | async-start | bytes 1048576 | tf_op jit(solution)/shard_map/all_to_all | solution.py:126
  468.5 15.8 %collective-permute-start.12 = (f32[3,32,512]{2,0,1:T(4,128)S(1)}, f32[3,32,512]{2,0,1:T(4,128)S(1)}, u32[]{:S(2)}, u32[]{:S(2)}) collective-permute-start(f32[3,32,512]{2,0,1:T(4,128)S(1)} %copy.152), channel_id=1, source_target_pairs={{0,16},{16,32},{32,48},{48,64},{64,80},{80,96},{96,112},{112,128},... | collective-permute-start | bytes 589832 | tf_op jit(solution)/shard_map/ppermute | solution.py:37
  473.1 11.2 %collective-permute-start.10 = (f32[2,3,1,512]{3,1,2,0:T(4,128)S(1)}, f32[2,3,1,512]{3,1,2,0:T(4,128)S(1)}, u32[]{:S(2)}, u32[]{:S(2)}) collective-permute-start(f32[2,3,1,512]{3,1,2,0:T(4,128)S(1)} %get-tuple-element.71), channel_id=1, source_target_pairs={{1,0},{2,1},{3,2},{4,3},{5,4},{6,5},{7,6},{8,7},{9,8},{10,9},{11,1... | collective-permute-start | bytes 36872 | tf_op jit(solution)/shard_map/ppermute | solution.py:29
  477.8 6.5 %collective-permute-start.11 = (f32[2,3,1,512]{3,1,2,0:T(4,128)S(1)}, f32[2,3,1,512]{3,1,2,0:T(4,128)S(1)}, u32[]{:S(2)}, u32[]{:S(2)}) collective-permute-start(f32[2,3,1,512]{3,1,2,0:T(4,128)S(1)} %get-tuple-element.70), channel_id=1, source_target_pairs={{0,1},{1,2},{2,3},{3,4},{4,5},{5,6},{6,7},{7,8},{8,9},{9,10},{10,1... | collective-permute-start | bytes 36872 | tf_op jit(solution)/shard_map/ppermute | solution.py:28
  484.1 1.0 copy-start.2
Sparse Core Ops, SparseCore 0:
  55.3 283.6 all-reduce.1
where the time goes:
time: 500 us; the launch traced here: 495 us
  waiting for transfers between devices  314 us (63%)
  starting transfers between devices  96 us (19%)
  blocking collectives  29.6 us (6%)
  matrix products  15.8 us (3%)
  between operations  14.8 us (3%)
  local copies, waits for them, and re-layouts  14.3 us (3%)
  other arithmetic  10.1 us (2%)
    psum x1, waiting for transfers between devices, spread(): return lax.psum(jnp.where(mine, shard, jnp.zeros_like(shard)), axis)  285 us
    ppermute x6, starting transfers between devices, padded_2(): after = lax.ppermute(leading, axis, down)  34.6 us
    all_to_all x1, blocking collectives, shards(): lax.all_to_all(stacked, 'tm', split_axis=2, concat_axis=1, tiled=True)  29.6 us
    ppermute x6, starting transfers between devices, padded_2(): before = lax.ppermute(last, axis, up)  22.2 us
    all_to_all x1, starting transfers between devices, shards(): lax.all_to_all(blocks, 'tm', split_axis=1, concat_axis=0, tiled=True)  16.5 us
    all_to_all x1, waiting for transfers between devices, shards(): lax.all_to_all(blocks, 'tm', split_axis=1, concat_axis=0, tiled=True)  14.6 us
    all_to_all x1, waiting for transfers between devices, shards(): lax.all_to_all(physical, 'tm', split_axis=0, concat_axis=1, tiled=True)  14.5 us
    dot_general x6, matrix products, cross_terms(): jnp.einsum('cd,...dxy->...cxy', react_off, center, precision=highest)  13.4 us
  transfers between devices with their start and end apart: 17, of which 3 were waited for; matrix products, arithmetic and copies ran while one was open for 3% of the time, Pallas kernels for 0%

commit v1 on v0

v1 whole, which is shorter than its diff:
```python
import functools

import jax
import jax.numpy as jnp
from jax import lax
from jax.experimental import pallas as pl
from jax.experimental.pallas import tpu as pltpu
from jax.sharding import PartitionSpec as P

ALPHA = 0.2
TM = 32
MESH = pl.DeviceIdType.MESH
F32 = jnp.float32


def place_of(tile, space):
    r, c = tile // 8, tile % 8
    odd = space % 2
    q = r + odd * (3 - 2 * r)
    half = c // 4
    y = (c % 4) + half * (3 - 2 * (c % 4))
    z = q + half * (7 - 2 * q)
    return y * 8 + z


def tile_of(tm, space):
    y, z = tm // 8, tm % 8
    half = z // 4
    q = z + half * (7 - 2 * z)
    c = half * 4 + y + half * (3 - 2 * y)
    odd = space % 2
    r = q + odd * (3 - 2 * q)
    return r * 8 + c


def kernel(
    b_hbm, prev_hbm, kappa_hbm, drift_s, react_s,
    out_u, out_res,
    bv, prev_v, kap, pack, held, prev_r, u5, u6, back5, back6, wn,
    row_s, row_r, col_s, col_r, edge_s, edge_r, coef,
    in_sem, a_send, a_recv, p_send, p_recv, h_send, h_recv, r5_send, r5_recv, r6_send, r6_recv, e_send, e_recv,
):
    me = lax.axis_index("tm")
    sp = lax.axis_index("space")
    spaces = lax.axis_size("space")
    tile = tile_of(me, sp)
    r, c = tile // 8, tile % 8

    load_b = pltpu.make_async_copy(b_hbm, bv, in_sem.at[0])
    load_k = pltpu.make_async_copy(kappa_hbm, kap, in_sem.at[1])
    load_p = pltpu.make_async_copy(prev_hbm.at[1], prev_v, in_sem.at[2])
    load_b.start()
    load_k.start()
    last = me == TM - 1

    @pl.when(last)
    def _():
        load_p.start()

    row_r[...] = jnp.zeros_like(row_r)
    edge_r[...] = jnp.zeros_like(edge_r)

    barrier = pltpu.get_barrier_semaphore()

    @pl.loop(1, TM)
    def _(o):
        pl.semaphore_signal(barrier, inc=1, device_id=((me + o) % TM, sp), device_id_type=MESH)

    @pl.when(sp > 0)
    def _():
        pl.semaphore_signal(barrier, inc=1, device_id=(me, sp - 1), device_id_type=MESH)

    @pl.when(sp < spaces - 1)
    def _():
        pl.semaphore_signal(barrier, inc=1, device_id=(me, sp + 1), device_id_type=MESH)

    lane = lax.broadcasted_iota(jnp.int32, (8, 128), 1)
    sub = lax.broadcasted_iota(jnp.int32, (8, 128), 0)
    odd = lane >= 64
    inner = lane % 64

    load_b.wait()

    @pl.loop(0, 16)
    def _(i):
        rr, cp = i // 4, i % 4
        rows = pl.ds(pl.multiple_of(rr * 8, 8), 8)
        cols = pl.ds(pl.multiple_of(cp * 128, 128), 128)
        for f in range(3):
            first = bv[0, f, rows, cols]
            second = bv[1, f, rows, cols]
            pack[rr * 8 + cp * 2, f] = jnp.where(odd, pltpu.roll(second, 64, 1), first)
            pack[rr * 8 + cp * 2 + 1, f] = jnp.where(odd, second, pltpu.roll(first, 64, 1))

    pl.semaphore_wait(barrier, TM - 1 + jnp.where(sp > 0, 1, 0) + jnp.where(sp < spaces - 1, 1, 0))

    def send_forward(o):
        p = (me + o) % TM
        return pltpu.make_async_remote_copy(
            src_ref=pack.at[tile_of(p, sp)], dst_ref=held.at[me], send_sem=a_send, recv_sem=a_recv,
            device_id=(p, sp), device_id_type=MESH)

    @pl.loop(1, TM)
    def _(o):
        send_forward(o).start()

    own = pltpu.make_async_copy(pack.at[tile], held.at[me], in_sem.at[3])
    own.start()

    def prev_part(t):
        rows = pl.ds(pl.multiple_of((t // 8) * 8, 8), 8)
        cols = pl.ds(pl.multiple_of(((t % 8) // 2) * 128, 128), 128)
        return prev_v.at[:, rows, cols]

    @pl.when(last)
    def _():
        load_p.wait()

        @pl.loop(0, TM - 1)
        def _(p):
            pltpu.make_async_remote_copy(
                src_ref=prev_part(tile_of(p, sp)), dst_ref=prev_r, send_sem=p_send, recv_sem=p_recv,
                device_id=(p, sp), device_id_type=MESH).start()

        mine = pltpu.make_async_copy(prev_part(tile), prev_r, in_sem.at[2])
        mine.start()
        mine.wait()

    load_k.wait()
    rows = pl.ds(pl.multiple_of(r * 8, 8), 8)
    cols = pl.ds(pl.multiple_of((c // 2) * 128, 128), 128)
    upper_half = (c % 2) == 1
    keep = jnp.where(upper_half, lane, 127 - lane) >= 64
    for f in range(3):
        k = kap[f, rows, cols]
        k = jnp.where(keep, k, pltpu.roll(k, 64, 1))
        g = 1.0 / (1.0 + 4.0 * k + react_s[f, f])
        g2 = g * g
        g4 = g2 * g2
        g8 = g4 * g4
        g16 = g8 * g8
        g32 = g16 * g16
        g64 = g32 * g32
        coef[0, f] = 0.5 * drift_s[f, 0] - k
        coef[1, f] = -0.5 * drift_s[f, 0] - k
        coef[2, f] = 0.5 * drift_s[f, 1] - k
        coef[3, f] = -0.5 * drift_s[f, 1] - k
        coef[4, f] = g
        coef[5, f] = ALPHA / (1.0 - ALPHA * g64)

    own.wait()
    pltpu.make_async_copy(pack.at[pl.ds(0, TM - 1)], held.at[pl.ds(0, TM - 1)], a_recv).wait()

    @pl.when(jnp.logical_not(last))
    def _():
        pltpu.make_async_copy(prev_r, prev_r, p_recv).wait()

    for f in range(3):
        p = prev_r[f]
        p = jnp.where(keep, p, pltpu.roll(p, 64, 1))
        held[0, f] = held[0, f] - ALPHA * jnp.where(odd, 0.0, p)

    zero = jnp.zeros((8, 128), F32)

    left = place_of(r * 8 + (c + 7) % 8, sp)
    right = place_of(r * 8 + (c + 1) % 8, sp)
    up_in = r > 0
    dn_in = r < 3
    has_up = jnp.logical_or(up_in, sp > 0)
    has_dn = jnp.logical_or(dn_in, sp < spaces - 1)
    up_tm = jnp.where(up_in, place_of(jnp.maximum(r - 1, 0) * 8 + c, sp), me)
    up_sp = jnp.where(up_in, sp, jnp.maximum(sp - 1, 0))
    dn_tm = jnp.where(dn_in, place_of(jnp.minimum(r + 1, 3) * 8 + c, sp), me)
    dn_sp = jnp.where(dn_in, sp, jnp.minimum(sp + 1, spaces - 1))

    def row_copy(j, way):
        return pltpu.make_async_remote_copy(
            src_ref=row_s.at[j, way], dst_ref=row_r.at[j, way], send_sem=h_send.at[j, way], recv_sem=h_recv.at[j, way],
            device_id=((up_tm, up_sp), (dn_tm, dn_sp))[way], device_id_type=MESH)

    def col_copy(j, way):
        return pltpu.make_async_remote_copy(
            src_ref=col_s.at[j, way], dst_ref=col_r.at[j, way], send_sem=h_send.at[j, 2 + way],
            recv_sem=h_recv.at[j, 2 + way], device_id=((left, right)[way], sp), device_id_type=MESH)

    def sweep(j, src, dst):
        def step(m, carry):
            out = []
            v = [src[m, f] for f in range(3)] if src is not None else None
            for f in range(3):
                g = coef[4, f]
                rest = held[m, f]
                if src is not None:
                    below = jnp.where(sub == 7, row_r[j, 0, f, pl.ds(m, 1), :], pltpu.roll(v[f], 7, 0))
                    above = jnp.where(sub == 0, row_r[j, 1, f, pl.ds(m, 1), :], pltpu.roll(v[f], 1, 0))
                    after = jnp.where(inner == 63, pltpu.roll(col_r[j, 0, f], 63 - m, 1), pltpu.roll(v[f], 127, 1))
                    before = jnp.where(inner == 0, pltpu.roll(col_r[j, 1, f], (128 - m) % 128, 1), pltpu.roll(v[f], 1, 1))
                    d, e = [i for i in range(3) if i != f]
                    off = (coef[0, f] * below + coef[1, f] * above + coef[2, f] * after + coef[3, f] * before
                           + (react_s[f, d] * v[d] + react_s[f, e] * v[e]))
                    rest = rest - off
                x = g * rest
                swapped = pltpu.roll(x, 64, 1)
                both = jnp.where(odd, x, swapped) + g * jnp.where(odd, swapped, x)
                total = both + (g * g) * carry[f]
                dst[m, f] = jnp.where(odd, total, x + g * carry[f])
                out.append(total)
            return tuple(out)

        ends = lax.fori_loop(0, TM, step, (zero, zero, zero))
        return tuple(coef[5, f] * ends[f] for f in range(3))

    def correct(j, dst, wrap, halo):
        def step(m, carry):
            out = []
            for f in range(3):
                g = coef[4, f]
                g2 = g * g
                w, lft, rgt = carry[3 * f:3 * f + 3]
                u = dst[m, f] + jnp.where(odd, g2, g) * w
                dst[m, f] = u
                w = g2 * w
                if halo:
                    row_s[j, 0, f, pl.ds(m, 1), :] = u[0:1]
                    row_s[j, 1, f, pl.ds(m, 1), :] = u[7:8]
                    here = inner == m
                    lft = jnp.where(here, pltpu.roll(u, m, 1), lft)
                    rgt = jnp.where(here, pltpu.roll(u, m + 65, 1), rgt)
                out += [w, lft, rgt]
            return tuple(out)

        start = []
        for f in range(3):
            start += [wrap[f], zero, zero]
        ends = lax.fori_loop(0, TM, step, tuple(start))
        if not halo:
            return
        for f in range(3):
            col_s[j, 0, f] = ends[3 * f + 1]
            col_s[j, 1, f] = ends[3 * f + 2]

        @pl.when(has_up)
        def _():
            row_copy(j, 0).start()

        @pl.when(has_dn)
        def _():
            row_copy(j, 1).start()

        col_copy(j, 0).start()
        col_copy(j, 1).start()

    def await_halo(j):
        @pl.when(has_dn)
        def _():
            row_copy(j, 0).wait_recv()

        @pl.when(has_up)
        def _():
            row_copy(j, 1).wait_recv()

        col_copy(j, 0).wait_recv()
        col_copy(j, 1).wait_recv()

    correct(0, u5, sweep(0, None, u5), True)

    @pl.loop(0, 4)
    def _(j):
        await_halo(j)
        correct(j + 1, u5, sweep(j, u5, u5), True)

    def send_back(o, src, dst, send_sem, recv_sem):
        p = (me + o) % TM
        return pltpu.make_async_remote_copy(
            src_ref=src.at[p], dst_ref=dst.at[tile], send_sem=send_sem, recv_sem=recv_sem,
            device_id=(p, sp), device_id_type=MESH)

    @pl.loop(1, TM)
    def _(o):
        send_back(o, u5, back5, r5_send, r5_recv).start()

    own5 = pltpu.make_async_copy(u5.at[me], back5.at[tile], in_sem.at[0])
    own5.start()

    await_halo(4)
    correct(4, u6, sweep(4, u5, u6), False)

    @pl.loop(1, TM)
    def _(o):
        send_back(o, u6, back6, r6_send, r6_recv).start()

    own6 = pltpu.make_async_copy(u6.at[me], back6.at[tile], in_sem.at[1])
    own6.start()

    own5.wait()
    own6.wait()
    some = pl.ds(0, TM - 1)
    pltpu.make_async_copy(u5.at[some], back5.at[some], r5_recv).wait()
    pltpu.make_async_copy(u6.at[some], back6.at[some], r6_recv).wait()

    first_step = jnp.where(me == 0, 1.0, 0.0)

    @pl.loop(0, 16)
    def _(i):
        rr, cp = i // 4, i % 4
        rows = pl.ds(pl.multiple_of(rr * 8, 8), 8)
        cols = pl.ds(pl.multiple_of(cp * 128, 128), 128)
        t = rr * 8 + cp * 2
        for f in range(3):
            a6, b6 = back6[t, f], back6[t + 1, f]
            a5, b5 = back5[t, f], back5[t + 1, f]
            n0 = jnp.where(odd, pltpu.roll(b6, 64, 1), a6)
            n1 = jnp.where(odd, b6, pltpu.roll(a6, 64, 1))
            o0 = jnp.where(odd, pltpu.roll(b5, 64, 1), a5)
            o1 = jnp.where(odd, b5, pltpu.roll(a5, 64, 1))
            out_u[0, f, rows, cols] = n0
            out_u[1, f, rows, cols] = n1
            wn[0, f, rows, cols] = o0 * (1.0 - first_step) - n0
            wn[1, f, rows, cols] = o1 - n1

    for s in range(2):
        for f in range(3):
            i = s * 3 + f
            edge_s[0, i:i + 1, :] = wn[s, f, 0:1, :]
            edge_s[1, i:i + 1, :] = wn[s, f, 31:32, :]

    def edge_copy(way):
        return pltpu.make_async_remote_copy(
            src_ref=edge_s.at[way], dst_ref=edge_r.at[way], send_sem=e_send.at[way], recv_sem=e_recv.at[way],
            device_id=(me, (jnp.maximum(sp - 1, 0), jnp.minimum(sp + 1, spaces - 1))[way]), device_id_type=MESH)

    @pl.when(sp > 0)
    def _():
        edge_copy(0).start()

    @pl.when(sp < spaces - 1)
    def _():
        edge_copy(1).start()

    @pl.when(sp < spaces - 1)
    def _():
        edge_copy(0).wait_recv()

    @pl.when(sp > 0)
    def _():
        edge_copy(1).wait_recv()

    tall = lax.broadcasted_iota(jnp.int32, (32, 512), 0)
    for s in range(2):
        w = [wn[s, f] for f in range(3)]
        for f in range(3):
            i = s * 3 + f
            k = kap[f]
            below = jnp.where(tall == 31, edge_r[0, i:i + 1, :], pltpu.roll(w[f], 31, 0))
            above = jnp.where(tall == 0, edge_r[1, i:i + 1, :], pltpu.roll(w[f], 1, 0))
            after = pltpu.roll(w[f], 511, 1)
            before = pltpu.roll(w[f], 1, 1)
            d, e = [n for n in range(3) if n != f]
            res = (0.5 * drift_s[f, 0] * (below - above) + 0.5 * drift_s[f, 1] * (after - before)
                   - k * (below + above + after + before) + (react_s[f, d] * w[d] + react_s[f, e] * w[e]))
            if s == 0:
                res = res + first_step * (bv[0, f] - (1.0 + 4.0 * k + react_s[f, f]) * out_u[0, f])
            out_res[s, f] = res

    pltpu.make_async_copy(pack.at[some], held.at[some], a_send).wait()
    pltpu.make_async_copy(u5.at[some], back5.at[some], r5_send).wait()
    pltpu.make_async_copy(u6.at[some], back6.at[some], r6_send).wait()

    @pl.when(last)
    def _():
        pltpu.make_async_copy(pack.at[some], held.at[some], p_send).wait()

    @pl.loop(0, 5)
    def _(j):
        @pl.when(has_up)
        def _():
            row_copy(j, 0).wait_send()

        @pl.when(has_dn)
        def _():
            row_copy(j, 1).wait_send()

        col_copy(j, 0).wait_send()
        col_copy(j, 1).wait_send()

    @pl.when(sp > 0)
    def _():
        edge_copy(0).wait_send()

    @pl.when(sp < spaces - 1)
    def _():
        edge_copy(1).wait_send()


def shards(previous, right_side, kappa, drift, reaction):
    anyspace = pl.BlockSpec(memory_space=pl.ANY)
    smem = pl.BlockSpec(memory_space=pltpu.SMEM)
    vmem = pl.BlockSpec(memory_space=pltpu.VMEM)
    shape = jax.ShapeDtypeStruct(right_side.shape, F32)
    dma = pltpu.SemaphoreType.DMA
    held = pltpu.VMEM((TM, 3, 8, 128), F32)
    return pl.pallas_call(
        kernel,
        out_shape=(shape, shape),
        in_specs=[anyspace, anyspace, anyspace, smem, smem],
        out_specs=(vmem, vmem),
        scratch_shapes=[
            pltpu.VMEM((2, 3, 32, 512), F32),
            pltpu.VMEM((3, 32, 512), F32),
            pltpu.VMEM((3, 32, 512), F32),
            held, held,
            pltpu.VMEM((3, 8, 128), F32),
            held, held, held, held,
            pltpu.VMEM((2, 3, 32, 512), F32),
            pltpu.VMEM((5, 2, 3, 32, 128), F32),
            pltpu.VMEM((5, 2, 3, 32, 128), F32),
            pltpu.VMEM((5, 2, 3, 8, 128), F32),
            pltpu.VMEM((5, 2, 3, 8, 128), F32),
            pltpu.VMEM((2, 8, 512), F32),
            pltpu.VMEM((2, 8, 512), F32),
            pltpu.VMEM((6, 3, 8, 128), F32),
            dma((4,)),
            dma, dma, dma, dma,
            dma((5, 4)), dma((5, 4)),
            dma, dma, dma, dma,
            dma((2,)), dma((2,)),
        ],
        compiler_params=pltpu.CompilerParams(
            collective_id=0, has_side_effects=True, vmem_limit_bytes=40 * 1024 * 1024),
    )(right_side, previous, kappa, drift, reaction)


def solution(mesh):
    in_specs = (
        P("tm", None, "space", None),
        P("tm", None, "space", None),
        P(None, "space", None),
        P(),
        P(),
    )
    out_specs = (P("tm", None, "space", None), P("tm", None, "space", None))
    return jax.shard_map(shards, mesh=mesh, in_specs=in_specs, out_specs=out_specs, check_vma=False)
```

time: 500 us -> 119 us (0.24)
  the two profiles are of different devices: /device:TPU:1 before, /device:TPU:55 now
where the time goes in v1:
time: 119 us
  Pallas kernels  113 us (95%)
  local copies, waits for them, and re-layouts  5.19 us (4%)
    pallas_call x1, Pallas kernels, shards(): pl.pallas_call(kernel, out_shape=(shape, shape), in_specs=[anyspace, anys...  113 us
    unnamed x11, local copies, waits for them, and re-layouts  5.19 us

profile of v1, /device:TPU:55, one launch (start us, length us, event | category | flops | bytes accessed | tf_op | source)
XLA Modules:
  0.0 118.8 jit_solution(4862365235808388548)
XLA Ops:
  0.6 0.0 copy-start.3
  0.6 0.8 copy.7.drift_s
  1.4 0.0 copy-done.3
  1.4 0.0 copy-start
  1.4 1.0 copy-done
  2.4 0.0 copy-start.1
  2.4 1.0 copy-done.1
  3.4 0.0 copy-start.2
  3.4 0.9 copy-done.2
  4.3 113.0 %shard_map.68 = (f32[2,3,32,512]{3,2,1,0:T(8,128)S(1)}, f32[2,3,32,512]{3,2,1,0:T(8,128)S(1)}) custom-call(f32[2,3,32,512]{3,2,1,0:T(8,128)S(1)} %copy-done, f32[2,3,32,512]{3,2,1,0:T(8,128)S(1)} %copy-done.1, f32[3,32,512]{2,1,0:T(8,128)S(1)} %copy-done.2, f32[3,2]{1,0:T(4,128)S(1)} %copy.7.drift_s, f32[3,3]{1,0:T(4,128)S(1)} %copy-done.3), custom_call_target="tpu_custom_call" | custom-call | tf_op jit(solution)/shard_map/pallas_call | solution.py:402
  117.3 0.7 copy.10
  118.1 0.7 copy.11
Async XLA Ops:
  0.6 0.8 copy-start.3
  1.4 1.0 copy-start
  2.4 1.0 copy-start.1
  3.4 0.9 copy-start.2

commit v2 on v1

v2 whole, which is shorter than its diff:
```python
import functools

import jax
import jax.numpy as jnp
from jax import lax
from jax.experimental import pallas as pl
from jax.experimental.pallas import tpu as pltpu
from jax.sharding import PartitionSpec as P

ALPHA = 0.2
TM = 32
MESH = pl.DeviceIdType.MESH
F32 = jnp.float32


def place_of(tile, space):
    r, c = tile // 8, tile % 8
    odd = space % 2
    q = r + odd * (3 - 2 * r)
    half = c // 4
    y = (c % 4) + half * (3 - 2 * (c % 4))
    z = q + half * (7 - 2 * q)
    return y * 8 + z


def tile_of(tm, space):
    y, z = tm // 8, tm % 8
    half = z // 4
    q = z + half * (7 - 2 * z)
    c = half * 4 + y + half * (3 - 2 * y)
    odd = space % 2
    r = q + odd * (3 - 2 * q)
    return r * 8 + c


HOPS = [(dy, dz) for dz in (4, 3, 5, 2, 6, 1, 7, 0) for dy in (2, 1, 3, 0) if (dy, dz) != (0, 0)]
UNROLL = 8


def kernel(
    b_hbm, prev_hbm, kappa_hbm, drift_s, react_s,
    out_u, out_res,
    bv, prev_v, kap, pack, msgs, held, prev_r, ua, ub, m5, m6, back5, back6, wn,
    row_s, row_r, col_s, col_r, edge_s, edge_r, coef, row_g, col_g,
    in_sem, a_send, a_recv, p_send, p_recv, h_send, h_recv, r5_send, r5_recv, r6_send, r6_recv, e_send, e_recv,
):
    me = lax.axis_index("tm")
    sp = lax.axis_index("space")
    spaces = lax.axis_size("space")
    tile = tile_of(me, sp)
    r, c = tile // 8, tile % 8
    my, mz = me // 8, me % 8
    peers = [((my + dy) % 4) * 8 + (mz + dz) % 8 for dy, dz in HOPS]

    load_b = pltpu.make_async_copy(b_hbm, bv, in_sem.at[0])
    load_k = pltpu.make_async_copy(kappa_hbm, kap, in_sem.at[1])
    load_p = pltpu.make_async_copy(prev_hbm.at[1], prev_v, in_sem.at[2])
    load_b.start()
    load_k.start()
    last = me == TM - 1

    @pl.when(last)
    def _():
        load_p.start()

    row_r[...] = jnp.zeros_like(row_r)
    edge_r[...] = jnp.zeros_like(edge_r)

    barrier = pltpu.get_barrier_semaphore()
    for p in peers:
        pl.semaphore_signal(barrier, inc=1, device_id=(p, sp), device_id_type=MESH)

    @pl.when(sp > 0)
    def _():
        pl.semaphore_signal(barrier, inc=1, device_id=(me, sp - 1), device_id_type=MESH)

    @pl.when(sp < spaces - 1)
    def _():
        pl.semaphore_signal(barrier, inc=1, device_id=(me, sp + 1), device_id_type=MESH)

    lane = lax.broadcasted_iota(jnp.int32, (8, 128), 1)
    sub = lax.broadcasted_iota(jnp.int32, (8, 128), 0)
    high = lane >= 64
    inner = lane % 64
    zero = jnp.zeros((8, 128), F32)

    def swap(x):
        return pltpu.roll(x, 64, 1)

    load_b.wait()

    @pl.loop(0, 4)
    def _(rr):
        rows = pl.ds(pl.multiple_of(rr * 8, 8), 8)
        for cp in range(4):
            cols = pl.ds(cp * 128, 128)
            for f in range(3):
                first = bv[0, f, rows, cols]
                second = bv[1, f, rows, cols]
                pack[rr * 8 + cp * 2, f] = jnp.where(high, swap(second), first)
                pack[rr * 8 + cp * 2 + 1, f] = jnp.where(high, second, swap(first))

    pl.semaphore_wait(barrier, TM - 1 + jnp.where(sp > 0, 1, 0) + jnp.where(sp < spaces - 1, 1, 0))

    def prev_part(t):
        rows = pl.ds(pl.multiple_of((t // 8) * 8, 8), 8)
        cols = pl.ds(pl.multiple_of(((t % 8) // 2) * 128, 128), 128)
        return prev_v.at[:, rows, cols]

    @pl.when(last)
    def _():
        load_p.wait()

        @pl.loop(0, TM - 1)
        def _(p):
            pltpu.make_async_remote_copy(
                src_ref=prev_part(tile_of(p, sp)), dst_ref=prev_r, send_sem=p_send, recv_sem=p_recv,
                device_id=(p, sp), device_id_type=MESH).start()

        mine = pltpu.make_async_copy(prev_part(tile), prev_r, in_sem.at[2])
        mine.start()
        mine.wait()

    for p in peers:
        pltpu.make_async_remote_copy(
            src_ref=pack.at[tile_of(p, sp)], dst_ref=msgs.at[me], send_sem=a_send, recv_sem=a_recv,
            device_id=(p, sp), device_id_type=MESH).start()
    own = pltpu.make_async_copy(pack.at[tile], msgs.at[me], in_sem.at[3])
    own.start()

    load_k.wait()
    rows = pl.ds(pl.multiple_of(r * 8, 8), 8)
    cols = pl.ds(pl.multiple_of((c // 2) * 128, 128), 128)
    upper_half = (c % 2) == 1
    keep = jnp.where(upper_half, lane, 127 - lane) >= 64
    ratio = []
    for f in range(3):
        k = kap[f, rows, cols]
        k = jnp.where(keep, k, swap(k))
        g = 1.0 / (1.0 + 4.0 * k + react_s[f, f])
        ratio.append(g)
        g2 = g * g
        g4 = g2 * g2
        g8 = g4 * g4
        g16 = g8 * g8
        g32 = g16 * g16
        below = g * (0.5 * drift_s[0, f] - k)
        above = g * (-0.5 * drift_s[0, f] - k)
        after = g * (0.5 * drift_s[1, f] - k)
        before = g * (-0.5 * drift_s[1, f] - k)
        d, e = [n for n in range(3) if n != f]
        coef[0, f] = jnp.where(sub == 7, 0.0, below)
        coef[1, f] = jnp.where(sub == 0, 0.0, above)
        coef[2, f] = jnp.where(inner == 63, 0.0, after)
        coef[3, f] = jnp.where(inner == 0, 0.0, before)
        coef[4, f] = g * react_s[f, d]
        coef[5, f] = g * react_s[f, e]
        coef[6, f] = jnp.where(sub == 7, below, jnp.where(sub == 0, above, 0.0))
        coef[7, f] = jnp.where(inner == 63, after, jnp.where(inner == 0, before, 0.0))
        coef[8, f] = g
        coef[9, f] = g32
        coef[10, f] = 1.0 / (1.0 - ALPHA * (g32 * g32))

    def power(i, carry):
        carry = list(carry)
        for u in range(UNROLL):
            m = i * UNROLL + u
            here = inner == m
            for f in range(3):
                w, lft, rgt = carry[3 * f:3 * f + 3]
                row_g[0, f, pl.ds(m, 1), :] = w[0:1]
                row_g[1, f, pl.ds(m, 1), :] = w[7:8]
                lft = jnp.where(here, pltpu.roll(w, m, 1), lft)
                rgt = jnp.where(here, pltpu.roll(w, m + 65, 1), rgt)
                carry[3 * f:3 * f + 3] = [w * coef[8, f], lft, rgt]
        return tuple(carry)

    start = []
    for f in range(3):
        start += [ratio[f], zero, zero]
    ends = lax.fori_loop(0, 32 // UNROLL, power, tuple(start))
    for f in range(3):
        col_g[0, f] = ends[3 * f + 1]
        col_g[1, f] = ends[3 * f + 2]

    left = place_of(r * 8 + (c + 7) % 8, sp)
    right = place_of(r * 8 + (c + 1) % 8, sp)
    up_in = r > 0
    dn_in = r < 3
    has_up = jnp.logical_or(up_in, sp > 0)
    has_dn = jnp.logical_or(dn_in, sp < spaces - 1)
    up_tm = jnp.where(up_in, place_of(jnp.maximum(r - 1, 0) * 8 + c, sp), me)
    up_sp = jnp.where(up_in, sp, jnp.maximum(sp - 1, 0))
    dn_tm = jnp.where(dn_in, place_of(jnp.minimum(r + 1, 3) * 8 + c, sp), me)
    dn_sp = jnp.where(dn_in, sp, jnp.minimum(sp + 1, spaces - 1))

    def row_copy(j, way):
        return pltpu.make_async_remote_copy(
            src_ref=row_s.at[j, way], dst_ref=row_r.at[j, way], send_sem=h_send.at[j, way], recv_sem=h_recv.at[j, way],
            device_id=((up_tm, up_sp), (dn_tm, dn_sp))[way], device_id_type=MESH)

    def col_copy(j, way):
        return pltpu.make_async_remote_copy(
            src_ref=col_s.at[j, way], dst_ref=col_r.at[j, way], send_sem=h_send.at[j, 2 + way],
            recv_sem=h_recv.at[j, 2 + way], device_id=((left, right)[way], sp), device_id_type=MESH)

    def carry_in(ends):
        out = []
        for f in range(3):
            end, other = ends[f], swap(ends[f])
            g32 = coef[9, f]
            final = (jnp.where(high, end, other) + g32 * jnp.where(high, other, end)) * coef[10, f]
            wrap = ALPHA * final
            out.append(jnp.where(high, other + g32 * wrap, wrap))
        return out

    def send_halo(j, came, lefts, rights):
        for f in range(3):
            row_s[j, 0, f] = row_s[j, 0, f] + row_g[0, f] * came[f][0:1]
            row_s[j, 1, f] = row_s[j, 1, f] + row_g[1, f] * came[f][7:8]
            col_s[j, 0, f] = lefts[f] + col_g[0, f] * jnp.where(high, came[f][:, 64:65], came[f][:, 0:1])
            col_s[j, 1, f] = rights[f] + col_g[1, f] * jnp.where(high, came[f][:, 127:128], came[f][:, 63:64])

        @pl.when(has_up)
        def _():
            row_copy(j, 0).start()

        @pl.when(has_dn)
        def _():
            row_copy(j, 1).start()

        col_copy(j, 0).start()
        col_copy(j, 1).start()

    def await_halo(j):
        @pl.when(has_dn)
        def _():
            row_copy(j, 0).wait_recv()

        @pl.when(has_up)
        def _():
            row_copy(j, 1).wait_recv()

        col_copy(j, 0).wait_recv()
        col_copy(j, 1).wait_recv()

    def pack_border(j, m, f, u, lft, rgt):
        here = inner == m
        row_s[j, 0, f, pl.ds(m, 1), :] = u[0:1]
        row_s[j, 1, f, pl.ds(m, 1), :] = u[7:8]
        return jnp.where(here, pltpu.roll(u, m, 1), lft), jnp.where(here, pltpu.roll(u, m + 65, 1), rgt)

    def interior(came, src, dst):
        def step(i, carry):
            carry = list(carry)
            for u in range(UNROLL):
                m = i * UNROLL + u
                v = []
                for f in range(3):
                    carry[f] = carry[f] * coef[8, f]
                    v.append(src[m, f] + carry[f])
                    if dst is not src:
                        src[m, f] = v[f]
                for f in range(3):
                    d, e = [n for n in range(3) if n != f]
                    off = (coef[0, f] * pltpu.roll(v[f], 7, 0) + coef[1, f] * pltpu.roll(v[f], 1, 0)
                           + coef[2, f] * pltpu.roll(v[f], 127, 1) + coef[3, f] * pltpu.roll(v[f], 1, 1)
                           + coef[4, f] * v[d] + coef[5, f] * v[e])
                    dst[m, f] = held[m, f] - off
            return tuple(carry)

        lax.fori_loop(0, 32 // UNROLL, step, tuple(came))

    def border_scan(j, dst, halo):
        def step(i, carry):
            carry = list(carry)
            for u in range(UNROLL):
                m = i * UNROLL + u
                for f in range(3):
                    before, lft, rgt = carry[3 * f:3 * f + 3]
                    rows = jnp.where(sub == 0, row_r[j, 1, f, pl.ds(m, 1), :], row_r[j, 0, f, pl.ds(m, 1), :])
                    cols = jnp.where(inner == 0, pltpu.roll(col_r[j, 1, f], (128 - m) % 128, 1),
                                     pltpu.roll(col_r[j, 0, f], 63 - m, 1))
                    x = dst[m, f] - (coef[6, f] * rows + coef[7, f] * cols)
                    now = x + coef[8, f] * before
                    dst[m, f] = now
                    if halo:
                        lft, rgt = pack_border(j + 1, m, f, now, lft, rgt)
                    carry[3 * f:3 * f + 3] = [now, lft, rgt]
            return tuple(carry)

        ends = lax.fori_loop(0, 32 // UNROLL, step, (zero,) * 9)
        return ends[0::3], ends[1::3], ends[2::3]

    own.wait()
    some = pl.ds(0, TM - 1)
    pltpu.make_async_copy(pack.at[some], msgs.at[some], a_recv).wait()

    @pl.when(jnp.logical_not(last))
    def _():
        pltpu.make_async_copy(prev_r, prev_r, p_recv).wait()

    for f in range(3):
        p = prev_r[f]
        p = jnp.where(keep, p, swap(p))
        msgs[0, f] = msgs[0, f] - ALPHA * jnp.where(high, 0.0, p)

    def first(i, carry):
        carry = list(carry)
        for u in range(UNROLL // 2):
            h = i * (UNROLL // 2) + u
            for f in range(3):
                before, lft, rgt = carry[3 * f:3 * f + 3]
                g = coef[8, f]
                a, b = msgs[h, f], msgs[16 + h, f]
                even = g * jnp.where(high, swap(b), a)
                odd = g * jnp.where(high, b, swap(a))
                held[2 * h, f] = even
                held[2 * h + 1, f] = odd
                now = even + g * before
                ua[2 * h, f] = now
                lft, rgt = pack_border(0, 2 * h, f, now, lft, rgt)
                now = odd + g * now
                ua[2 * h + 1, f] = now
                lft, rgt = pack_border(0, 2 * h + 1, f, now, lft, rgt)
                carry[3 * f:3 * f + 3] = [now, lft, rgt]
        return tuple(carry)

    ends = lax.fori_loop(0, 32 // UNROLL, first, (zero,) * 9)
    came = carry_in(ends[0::3])
    send_halo(0, came, ends[1::3], ends[2::3])

    def sweep(j, came):
        interior(came, ua, ua)
        await_halo(j)
        ends, lefts, rights = border_scan(j, ua, True)
        came = carry_in(ends)
        send_halo(j + 1, came, lefts, rights)
        return tuple(came)

    came = lax.fori_loop(0, 4, sweep, tuple(came))

    def to_messages(src, dst, came):
        def step(i, carry):
            carry = list(carry)
            for u in range(UNROLL // 2):
                h = i * (UNROLL // 2) + u
                for f in range(3):
                    even, odd = src[2 * h, f], src[2 * h + 1, f]
                    if came is not None:
                        w = carry[f] * coef[8, f]
                        even = even + w
                        w = w * coef[8, f]
                        odd = odd + w
                        carry[f] = w
                    dst[h, f] = jnp.where(high, swap(odd), even)
                    dst[16 + h, f] = jnp.where(high, odd, swap(even))
            return tuple(carry)

        lax.fori_loop(0, 32 // UNROLL, step, tuple(came) if came is not None else ())

    def send_back(src, dst, send_sem, recv_sem, own_sem):
        for p in peers:
            pltpu.make_async_remote_copy(
                src_ref=src.at[p], dst_ref=dst.at[tile], send_sem=send_sem, recv_sem=recv_sem,
                device_id=(p, sp), device_id_type=MESH).start()
        own = pltpu.make_async_copy(src.at[me], dst.at[tile], own_sem)
        own.start()
        return own

    interior(came, ua, ub)
    to_messages(ua, m5, None)
    own5 = send_back(m5, back5, r5_send, r5_recv, in_sem.at[0])
    await_halo(4)
    ends, _, _ = border_scan(4, ub, False)
    to_messages(ub, m6, carry_in(ends))
    own6 = send_back(m6, back6, r6_send, r6_recv, in_sem.at[1])

    own5.wait()
    own6.wait()
    pltpu.make_async_copy(m5.at[some], back5.at[some], r5_recv).wait()
    pltpu.make_async_copy(m6.at[some], back6.at[some], r6_recv).wait()

    first_step = jnp.where(me == 0, 1.0, 0.0)

    @pl.loop(0, 4)
    def _(rr):
        rows = pl.ds(pl.multiple_of(rr * 8, 8), 8)
        for cp in range(4):
            cols = pl.ds(cp * 128, 128)
            t = rr * 8 + cp * 2
            for f in range(3):
                a6, b6 = back6[t, f], back6[t + 1, f]
                a5, b5 = back5[t, f], back5[t + 1, f]
                n0 = jnp.where(high, swap(b6), a6)
                n1 = jnp.where(high, b6, swap(a6))
                o0 = jnp.where(high, swap(b5), a5)
                o1 = jnp.where(high, b5, swap(a5))
                out_u[0, f, rows, cols] = n0
                out_u[1, f, rows, cols] = n1
                wn[0, f, rows, cols] = o0 * (1.0 - first_step) - n0
                wn[1, f, rows, cols] = o1 - n1

    for s in range(2):
        for f in range(3):
            i = s * 3 + f
            edge_s[0, i:i + 1, :] = wn[s, f, 0:1, :]
            edge_s[1, i:i + 1, :] = wn[s, f, 31:32, :]

    def edge_copy(way):
        return pltpu.make_async_remote_copy(
            src_ref=edge_s.at[way], dst_ref=edge_r.at[way], send_sem=e_send.at[way], recv_sem=e_recv.at[way],
            device_id=(me, (jnp.maximum(sp - 1, 0), jnp.minimum(sp + 1, spaces - 1))[way]), device_id_type=MESH)

    @pl.when(sp > 0)
    def _():
        edge_copy(0).start()

    @pl.when(sp < spaces - 1)
    def _():
        edge_copy(1).start()

    @pl.when(sp < spaces - 1)
    def _():
        edge_copy(0).wait_recv()

    @pl.when(sp > 0)
    def _():
        edge_copy(1).wait_recv()

    tall = lax.broadcasted_iota(jnp.int32, (32, 512), 0)
    for s in range(2):
        w = [wn[s, f] for f in range(3)]
        for f in range(3):
            i = s * 3 + f
            k = kap[f]
            below = jnp.where(tall == 31, edge_r[0, i:i + 1, :], pltpu.roll(w[f], 31, 0))
            above = jnp.where(tall == 0, edge_r[1, i:i + 1, :], pltpu.roll(w[f], 1, 0))
            after = pltpu.roll(w[f], 511, 1)
            before = pltpu.roll(w[f], 1, 1)
            d, e = [n for n in range(3) if n != f]
            res = (0.5 * drift_s[0, f] * (below - above) + 0.5 * drift_s[1, f] * (after - before)
                   - k * (below + above + after + before) + (react_s[f, d] * w[d] + react_s[f, e] * w[e]))
            if s == 0:
                res = res + first_step * (bv[0, f] - (1.0 + 4.0 * k + react_s[f, f]) * out_u[0, f])
            out_res[s, f] = res

    pltpu.make_async_copy(pack.at[some], msgs.at[some], a_send).wait()
    pltpu.make_async_copy(m5.at[some], back5.at[some], r5_send).wait()
    pltpu.make_async_copy(m6.at[some], back6.at[some], r6_send).wait()

    @pl.when(last)
    def _():
        pltpu.make_async_copy(pack.at[some], msgs.at[some], p_send).wait()

    @pl.loop(0, 5)
    def _(j):
        @pl.when(has_up)
        def _():
            row_copy(j, 0).wait_send()

        @pl.when(has_dn)
        def _():
            row_copy(j, 1).wait_send()

        col_copy(j, 0).wait_send()
        col_copy(j, 1).wait_send()

    @pl.when(sp > 0)
    def _():
        edge_copy(0).wait_send()

    @pl.when(sp < spaces - 1)
    def _():
        edge_copy(1).wait_send()


def shards(previous, right_side, kappa, drift, reaction):
    hbm = pl.BlockSpec(memory_space=pltpu.HBM)
    smem = pl.BlockSpec(memory_space=pltpu.SMEM)
    vmem = pl.BlockSpec(memory_space=pltpu.VMEM)
    shape = jax.ShapeDtypeStruct(right_side.shape, F32)
    dma = pltpu.SemaphoreType.DMA
    held = pltpu.VMEM((TM, 3, 8, 128), F32)
    natural = pltpu.VMEM((2, 3, 32, 512), F32)
    return pl.pallas_call(
        kernel,
        out_shape=(shape, shape),
        in_specs=[hbm, hbm, hbm, smem, smem],
        out_specs=(vmem, vmem),
        scratch_shapes=[
            natural,
            pltpu.VMEM((3, 32, 512), F32),
            pltpu.VMEM((3, 32, 512), F32),
            held, held, held,
            pltpu.VMEM((3, 8, 128), F32),
            held, held, held, held, held, held,
            natural,
            pltpu.VMEM((5, 2, 3, 32, 128), F32),
            pltpu.VMEM((5, 2, 3, 32, 128), F32),
            pltpu.VMEM((5, 2, 3, 8, 128), F32),
            pltpu.VMEM((5, 2, 3, 8, 128), F32),
            pltpu.VMEM((2, 8, 512), F32),
            pltpu.VMEM((2, 8, 512), F32),
            pltpu.VMEM((11, 3, 8, 128), F32),
            pltpu.VMEM((2, 3, 32, 128), F32),
            pltpu.VMEM((2, 3, 8, 128), F32),
            dma((4,)),
            dma, dma, dma, dma,
            dma((5, 4)), dma((5, 4)),
            dma, dma, dma, dma,
            dma((2,)), dma((2,)),
        ],
        compiler_params=pltpu.CompilerParams(
            collective_id=0, has_side_effects=True, vmem_limit_bytes=40 * 1024 * 1024),
    )(right_side, previous, kappa, drift.T, reaction)


def solution(mesh):
    in_specs = (
        P("tm", None, "space", None),
        P("tm", None, "space", None),
        P(None, "space", None),
        P(),
        P(),
    )
    out_specs = (P("tm", None, "space", None), P("tm", None, "space", None))
    return jax.shard_map(shards, mesh=mesh, in_specs=in_specs, out_specs=out_specs, check_vma=False)
```

time: 119 us -> 87.8 us (0.74)
  the two profiles are of different devices: /device:TPU:55 before, /device:TPU:1 now
where the time goes in v2:
time: 87.8 us; the launch traced here: 86.8 us
  Pallas kernels  80.4 us (92%)
  local copies, waits for them, and re-layouts  5.76 us (7%)
    pallas_call x1, Pallas kernels, shards(): pl.pallas_call(kernel, out_shape=(shape, shape), in_specs=[hbm, hbm, hbm,...  80.4 us
    unnamed x12, local copies, waits for them, and re-layouts  5.76 us

profile of v2, /device:TPU:1, one launch (start us, length us, event | category | flops | bytes accessed | tf_op | source)
XLA Modules:
  0.0 86.8 jit_solution(11155444005478398204)
XLA Ops:
  0.6 0.0 copy-start.4
  0.6 0.7 copy-done.4
  1.3 0.0 copy-start
  1.3 1.0 %copy-done = f32[2,3,32,512]{3,2,1,0:T(8,128)S(1)} copy-done((f32[2,3,32,512]{3,2,1,0:T(8,128)S(1)}, f32[2,3,32,512]{3,2,1,0:T(8,128)}, u32[]{:S(2)}) %copy-start) | copy-done | bytes 393240
  2.3 0.0 copy-start.1
  2.3 1.0 %copy-done.1 = f32[2,3,32,512]{3,2,1,0:T(8,128)S(1)} copy-done((f32[2,3,32,512]{3,2,1,0:T(8,128)S(1)}, f32[2,3,32,512]{3,2,1,0:T(8,128)}, u32[]{:S(2)}) %copy-start.1) | copy-done | bytes 393240
  3.3 0.0 copy-start.2
  3.3 0.9 %copy-done.2 = f32[3,32,512]{2,1,0:T(8,128)S(1)} copy-done((f32[3,32,512]{2,1,0:T(8,128)S(1)}, f32[3,32,512]{2,1,0:T(8,128)}, u32[]{:S(2)}) %copy-start.2) | copy-done | bytes 196632
  4.2 0.0 copy-start.3
  4.2 0.7 copy-done.3
  4.9 80.4 %shard_map.68 = (f32[2,3,32,512]{3,2,1,0:T(8,128)S(1)}, f32[2,3,32,512]{3,2,1,0:T(8,128)S(1)}) custom-call(f32[2,3,32,512]{3,2,1,0:T(8,128)S(1)} %copy-done, f32[2,3,32,512]{3,2,1,0:T(8,128)S(1)} %copy-done.1, f32[3,32,512]{2,1,0:T(8,128)S(1)} %copy-done.2, f32[2,3]{1,0:T(2,128)S(1)} %bitcast.1, f32[3,3]{1,0:T(4,128)S(1)} %copy-done.3), custom_call_target="tpu_custom_call" | custom-call | tf_op jit(solution)/shard_map/pallas_call | solution.py:486
  85.3 0.7 copy.9
  86.0 0.7 copy.10
Async XLA Ops:
  0.6 0.7 copy-start.4
  1.3 1.0 %copy-start = (f32[2,3,32,512]{3,2,1,0:T(8,128)S(1)}, f32[2,3,32,512]{3,2,1,0:T(8,128)}, u32[]{:S(2)}) copy-start(f32[2,3,32,512]{3,2,1,0:T(8,128)} %b_hbm.1) | copy-start | bytes 1179652
  2.3 1.0 %copy-start.1 = (f32[2,3,32,512]{3,2,1,0:T(8,128)S(1)}, f32[2,3,32,512]{3,2,1,0:T(8,128)}, u32[]{:S(2)}) copy-start(f32[2,3,32,512]{3,2,1,0:T(8,128)} %prev_hbm.1) | copy-start | bytes 1179652
  3.3 0.9 %copy-start.2 = (f32[3,32,512]{2,1,0:T(8,128)S(1)}, f32[3,32,512]{2,1,0:T(8,128)}, u32[]{:S(2)}) copy-start(f32[3,32,512]{2,1,0:T(8,128)} %kappa_hbm.1) | copy-start | bytes 589828
  4.2 0.7 copy-start.3

commit v3 on v2

--- a/solution.py
+++ b/solution.py
@@ -40,8 +40,8 @@
 def kernel(
     b_hbm, prev_hbm, kappa_hbm, drift_s, react_s,
     out_u, out_res,
-    bv, prev_v, kap, pack, msgs, held, prev_r, ua, ub, m5, m6, back5, back6, wn,
-    row_s, row_r, col_s, col_r, edge_s, edge_r, coef, row_g, col_g,
+    bv, prev_v, kap, pack, msgs, held, prev_s, prev_r, ua, ub, m5, m6, back5, back6, wn,
+    row_s, row_r, col_s, col_r, edge_s, edge_r, edge_n, coef, row_g, col_g,
     in_sem, a_send, a_recv, p_send, p_recv, h_send, h_recv, r5_send, r5_recv, r6_send, r6_recv, e_send, e_recv,
 ):
     me = lax.axis_index("tm")
@@ -65,6 +65,7 @@
 
     row_r[...] = jnp.zeros_like(row_r)
     edge_r[...] = jnp.zeros_like(edge_r)
+    edge_s[...] = jnp.zeros_like(edge_s)
 
     barrier = pltpu.get_barrier_semaphore()
     for p in peers:
@@ -72,11 +73,16 @@
 
     @pl.when(sp > 0)
     def _():
-        pl.semaphore_signal(barrier, inc=1, device_id=(me, sp - 1), device_id_type=MESH)
+        for n in range(8):
+            pl.semaphore_signal(barrier, inc=1, device_id=(place_of(24 + n, sp - 1), sp - 1), device_id_type=MESH)
 
     @pl.when(sp < spaces - 1)
     def _():
-        pl.semaphore_signal(barrier, inc=1, device_id=(me, sp + 1), device_id_type=MESH)
+        for n in range(8):
+            pl.semaphore_signal(barrier, inc=1, device_id=(place_of(n, sp + 1), sp + 1), device_id_type=MESH)
+
+    edge_up = jnp.logical_and(r == 0, sp > 0)
+    edge_dn = jnp.logical_and(r == 3, sp < spaces - 1)
 
     lane = lax.broadcasted_iota(jnp.int32, (8, 128), 1)
     sub = lax.broadcasted_iota(jnp.int32, (8, 128), 0)
@@ -86,6 +92,15 @@
 
     def swap(x):
         return pltpu.roll(x, 64, 1)
+
+    def fold_low(x):
+        return jnp.where(high, pltpu.roll(swap(x), 4, 0), x)[0:4]
+
+    def fold_high(x):
+        return jnp.where(high, pltpu.roll(x, 4, 0), swap(x))[0:4]
+
+    def unfold(x):
+        return jnp.concatenate([x, swap(x)], axis=0)
 
     load_b.wait()
 
@@ -100,24 +115,26 @@
                 pack[rr * 8 + cp * 2, f] = jnp.where(high, swap(second), first)
                 pack[rr * 8 + cp * 2 + 1, f] = jnp.where(high, second, swap(first))
 
-    pl.semaphore_wait(barrier, TM - 1 + jnp.where(sp > 0, 1, 0) + jnp.where(sp < spaces - 1, 1, 0))
-
-    def prev_part(t):
-        rows = pl.ds(pl.multiple_of((t // 8) * 8, 8), 8)
-        cols = pl.ds(pl.multiple_of(((t % 8) // 2) * 128, 128), 128)
-        return prev_v.at[:, rows, cols]
+    pl.semaphore_wait(barrier, TM - 1 + jnp.where(edge_up, TM, 0) + jnp.where(edge_dn, TM, 0))
 
     @pl.when(last)
     def _():
         load_p.wait()
 
-        @pl.loop(0, TM - 1)
-        def _(p):
+        @pl.loop(0, 4)
+        def _(rr):
+            rows = pl.ds(pl.multiple_of(rr * 8, 8), 8)
+            for cp in range(4):
+                for f in range(3):
+                    v = prev_v[f, rows, cp * 128:cp * 128 + 128]
+                    prev_s[rr * 8 + cp * 2, f] = fold_low(v)
+                    prev_s[rr * 8 + cp * 2 + 1, f] = fold_high(v)
+
+        for p in peers:
             pltpu.make_async_remote_copy(
-                src_ref=prev_part(tile_of(p, sp)), dst_ref=prev_r, send_sem=p_send, recv_sem=p_recv,
+                src_ref=prev_s.at[tile_of(p, sp)], dst_ref=prev_r, send_sem=p_send, recv_sem=p_recv,
                 device_id=(p, sp), device_id_type=MESH).start()
-
-        mine = pltpu.make_async_copy(prev_part(tile), prev_r, in_sem.at[2])
+        mine = pltpu.make_async_copy(prev_s.at[tile], prev_r, in_sem.at[2])
         mine.start()
         mine.wait()
 
@@ -216,10 +233,13 @@
 
     def send_halo(j, came, lefts, rights):
         for f in range(3):
+            col_s[j, 0, f] = lefts[f] + col_g[0, f] * jnp.where(high, came[f][:, 64:65], came[f][:, 0:1])
+            col_s[j, 1, f] = rights[f] + col_g[1, f] * jnp.where(high, came[f][:, 127:128], came[f][:, 63:64])
+        col_copy(j, 0).start()
+        col_copy(j, 1).start()
+        for f in range(3):
             row_s[j, 0, f] = row_s[j, 0, f] + row_g[0, f] * came[f][0:1]
             row_s[j, 1, f] = row_s[j, 1, f] + row_g[1, f] * came[f][7:8]
-            col_s[j, 0, f] = lefts[f] + col_g[0, f] * jnp.where(high, came[f][:, 64:65], came[f][:, 0:1])
-            col_s[j, 1, f] = rights[f] + col_g[1, f] * jnp.where(high, came[f][:, 127:128], came[f][:, 63:64])
 
         @pl.when(has_up)
         def _():
@@ -228,9 +248,6 @@
         @pl.when(has_dn)
         def _():
             row_copy(j, 1).start()
-
-        col_copy(j, 0).start()
-        col_copy(j, 1).start()
 
     def await_halo(j):
         @pl.when(has_dn)
@@ -301,8 +318,7 @@
         pltpu.make_async_copy(prev_r, prev_r, p_recv).wait()
 
     for f in range(3):
-        p = prev_r[f]
-        p = jnp.where(keep, p, swap(p))
+        p = unfold(prev_r[f])
         msgs[0, f] = msgs[0, f] - ALPHA * jnp.where(high, 0.0, p)
 
     def first(i, carry):
@@ -340,24 +356,35 @@
 
     came = lax.fori_loop(0, 4, sweep, tuple(came))
 
-    def to_messages(src, dst, came):
-        def step(i, carry):
-            carry = list(carry)
-            for u in range(UNROLL // 2):
-                h = i * (UNROLL // 2) + u
-                for f in range(3):
-                    even, odd = src[2 * h, f], src[2 * h + 1, f]
-                    if came is not None:
-                        w = carry[f] * coef[8, f]
-                        even = even + w
-                        w = w * coef[8, f]
-                        odd = odd + w
-                        carry[f] = w
-                    dst[h, f] = jnp.where(high, swap(odd), even)
-                    dst[16 + h, f] = jnp.where(high, odd, swap(even))
-            return tuple(carry)
-
-        lax.fori_loop(0, 32 // UNROLL, step, tuple(came) if came is not None else ())
+    def fold_even(i, carry):
+        for u in range(UNROLL // 2):
+            h = i * (UNROLL // 2) + u
+            for f in range(3):
+                even = ua[2 * h, f]
+                m5[h, f] = fold_low(even)
+                m5[16 + h, f] = fold_high(even)
+        return carry
+
+    def to_messages(i, carry):
+        carry = list(carry)
+        for u in range(UNROLL // 2):
+            h = i * (UNROLL // 2) + u
+            for f in range(3):
+                w = carry[f] * coef[8, f]
+                even = ub[2 * h, f] + w
+                w = w * coef[8, f]
+                odd = ub[2 * h + 1, f] + w
+                carry[f] = w
+                fifth = ua[2 * h, f]
+                one = jnp.where(high, swap(odd), even)
+                two = jnp.where(high, odd, swap(even))
+                m6[h, f] = one
+                m6[16 + h, f] = two
+                one = jnp.where(high, 0.0, fifth) * jnp.where(h == 0, 0.0, 1.0) - one
+                two = jnp.where(high, 0.0, swap(fifth)) - two
+                edge_s[h, f:f + 1, :] = jnp.where(r == 0, one[0:1], one[7:8])
+                edge_s[16 + h, f:f + 1, :] = jnp.where(r == 0, two[0:1], two[7:8])
+        return tuple(carry)
 
     def send_back(src, dst, send_sem, recv_sem, own_sem):
         for p in peers:
@@ -369,12 +396,27 @@
         return own
 
     interior(came, ua, ub)
-    to_messages(ua, m5, None)
+    lax.fori_loop(0, 32 // UNROLL, fold_even, 0)
     own5 = send_back(m5, back5, r5_send, r5_recv, in_sem.at[0])
     await_halo(4)
     ends, _, _ = border_scan(4, ub, False)
-    to_messages(ub, m6, carry_in(ends))
+    lax.fori_loop(0, 32 // UNROLL, to_messages, tuple(carry_in(ends)))
     own6 = send_back(m6, back6, r6_send, r6_recv, in_sem.at[1])
+
+    def send_edge(way):
+        for o in range(TM):
+            p = (me + o) % TM
+            pltpu.make_async_remote_copy(
+                src_ref=edge_s.at[p], dst_ref=edge_r.at[way, c], send_sem=e_send, recv_sem=e_recv.at[way],
+                device_id=(p, sp - 1 + 2 * way), device_id_type=MESH).start()
+
+    @pl.when(edge_up)
+    def _():
+        send_edge(0)
+
+    @pl.when(edge_dn)
+    def _():
+        send_edge(1)
 
     own5.wait()
     own6.wait()
@@ -391,58 +433,46 @@
             t = rr * 8 + cp * 2
             for f in range(3):
                 a6, b6 = back6[t, f], back6[t + 1, f]
-                a5, b5 = back5[t, f], back5[t + 1, f]
                 n0 = jnp.where(high, swap(b6), a6)
                 n1 = jnp.where(high, b6, swap(a6))
-                o0 = jnp.where(high, swap(b5), a5)
-                o1 = jnp.where(high, b5, swap(a5))
+                o0 = jnp.where(high, swap(unfold(back5[t + 1, f])), unfold(back5[t, f]))
                 out_u[0, f, rows, cols] = n0
                 out_u[1, f, rows, cols] = n1
                 wn[0, f, rows, cols] = o0 * (1.0 - first_step) - n0
-                wn[1, f, rows, cols] = o1 - n1
-
-    for s in range(2):
-        for f in range(3):
-            i = s * 3 + f
-            edge_s[0, i:i + 1, :] = wn[s, f, 0:1, :]
-            edge_s[1, i:i + 1, :] = wn[s, f, 31:32, :]
-
-    def edge_copy(way):
-        return pltpu.make_async_remote_copy(
-            src_ref=edge_s.at[way], dst_ref=edge_r.at[way], send_sem=e_send.at[way], recv_sem=e_recv.at[way],
-            device_id=(me, (jnp.maximum(sp - 1, 0), jnp.minimum(sp + 1, spaces - 1))[way]), device_id_type=MESH)
+                wn[1, f, rows, cols] = -n1
+
+    @pl.when(sp < spaces - 1)
+    def _():
+        pltpu.make_async_copy(edge_r.at[0], edge_r.at[0], e_recv.at[0]).wait()
 
     @pl.when(sp > 0)
     def _():
-        edge_copy(0).start()
-
-    @pl.when(sp < spaces - 1)
-    def _():
-        edge_copy(1).start()
-
-    @pl.when(sp < spaces - 1)
-    def _():
-        edge_copy(0).wait_recv()
-
-    @pl.when(sp > 0)
-    def _():
-        edge_copy(1).wait_recv()
+        pltpu.make_async_copy(edge_r.at[1], edge_r.at[1], e_recv.at[1]).wait()
+
+    high4 = lax.broadcasted_iota(jnp.int32, (4, 128), 1) >= 64
+    for way in range(2):
+        for cp in range(4):
+            a, b = edge_r[way, 2 * cp], edge_r[way, 2 * cp + 1]
+            edge_n[way, 0, :, cp * 128:cp * 128 + 128] = jnp.where(high4, swap(b), a)
+            edge_n[way, 1, :, cp * 128:cp * 128 + 128] = jnp.where(high4, b, swap(a))
 
     tall = lax.broadcasted_iota(jnp.int32, (32, 512), 0)
     for s in range(2):
         w = [wn[s, f] for f in range(3)]
         for f in range(3):
-            i = s * 3 + f
             k = kap[f]
-            below = jnp.where(tall == 31, edge_r[0, i:i + 1, :], pltpu.roll(w[f], 31, 0))
-            above = jnp.where(tall == 0, edge_r[1, i:i + 1, :], pltpu.roll(w[f], 1, 0))
+            below = jnp.where(tall == 31, edge_n[0, s, f:f + 1, :], pltpu.roll(w[f], 31, 0))
+            above = jnp.where(tall == 0, edge_n[1, s, f:f + 1, :], pltpu.roll(w[f], 1, 0))
             after = pltpu.roll(w[f], 511, 1)
             before = pltpu.roll(w[f], 1, 1)
             d, e = [n for n in range(3) if n != f]
             res = (0.5 * drift_s[0, f] * (below - above) + 0.5 * drift_s[1, f] * (after - before)
                    - k * (below + above + after + before) + (react_s[f, d] * w[d] + react_s[f, e] * w[e]))
+            own = bv[s, f] - (1.0 + 4.0 * k + react_s[f, f]) * out_u[s, f]
             if s == 0:
-                res = res + first_step * (bv[0, f] - (1.0 + 4.0 * k + react_s[f, f]) * out_u[0, f])
+                res = res + first_step * own
+            else:
+                res = res + (own + out_u[0, f])
             out_res[s, f] = res
 
     pltpu.make_async_copy(pack.at[some], msgs.at[some], a_send).wait()
@@ -451,7 +481,7 @@
 
     @pl.when(last)
     def _():
-        pltpu.make_async_copy(pack.at[some], msgs.at[some], p_send).wait()
+        pltpu.make_async_copy(prev_s.at[some], prev_s.at[some], p_send).wait()
 
     @pl.loop(0, 5)
     def _(j):
@@ -466,13 +496,9 @@
         col_copy(j, 0).wait_send()
         col_copy(j, 1).wait_send()
 
-    @pl.when(sp > 0)
-    def _():
-        edge_copy(0).wait_send()
-
-    @pl.when(sp < spaces - 1)
-    def _():
-        edge_copy(1).wait_send()
+    @pl.when(jnp.logical_or(edge_up, edge_dn))
+    def _():
+        pltpu.make_async_copy(edge_s, edge_s, e_send).wait()
 
 
 def shards(previous, right_side, kappa, drift, reaction):
@@ -482,6 +508,7 @@
     shape = jax.ShapeDtypeStruct(right_side.shape, F32)
     dma = pltpu.SemaphoreType.DMA
     held = pltpu.VMEM((TM, 3, 8, 128), F32)
+    folded = pltpu.VMEM((TM, 3, 4, 128), F32)
     natural = pltpu.VMEM((2, 3, 32, 512), F32)
     return pl.pallas_call(
         kernel,
@@ -493,15 +520,16 @@
             pltpu.VMEM((3, 32, 512), F32),
             pltpu.VMEM((3, 32, 512), F32),
             held, held, held,
-            pltpu.VMEM((3, 8, 128), F32),
-            held, held, held, held, held, held,
+            folded, pltpu.VMEM((3, 4, 128), F32),
+            held, held, folded, held, folded, held,
             natural,
             pltpu.VMEM((5, 2, 3, 32, 128), F32),
             pltpu.VMEM((5, 2, 3, 32, 128), F32),
             pltpu.VMEM((5, 2, 3, 8, 128), F32),
             pltpu.VMEM((5, 2, 3, 8, 128), F32),
-            pltpu.VMEM((2, 8, 512), F32),
-            pltpu.VMEM((2, 8, 512), F32),
+            pltpu.VMEM((TM, 4, 128), F32),
+            pltpu.VMEM((2, 8, 4, 128), F32),
+            pltpu.VMEM((2, 2, 4, 512), F32),
             pltpu.VMEM((11, 3, 8, 128), F32),
             pltpu.VMEM((2, 3, 32, 128), F32),
             pltpu.VMEM((2, 3, 8, 128), F32),
@@ -509,10 +537,10 @@
             dma, dma, dma, dma,
             dma((5, 4)), dma((5, 4)),
             dma, dma, dma, dma,
-            dma((2,)), dma((2,)),
+            dma, dma((2,)),
         ],
         compiler_params=pltpu.CompilerParams(
-            collective_id=0, has_side_effects=True, vmem_limit_bytes=40 * 1024 * 1024),
+            collective_id=0, has_side_effects=True, vmem_limit_bytes=56 * 1024 * 1024),
     )(right_side, previous, kappa, drift.T, reaction)
 
 

time: 87.8 us -> 75.9 us (0.86)
  Pallas kernels: 80.4 us -> 72.5 us
  local copies, waits for them, and re-layouts: 5.76 us -> 2.58 us
    pallas_call x1, Pallas kernels: 80.4 us -> 72.5 us  [shards(): pl.pallas_call(kernel, out_shape=(shape, shape), in_specs=[hbm, hbm, hbm,...]
    unnamed x12 -> x4, local copies, waits for them, and re-layouts: 5.76 us -> 2.58 us
where the time goes in v3:
time: 75.9 us; the launch traced here: 75.8 us
  Pallas kernels  72.5 us (96%)
  local copies, waits for them, and re-layouts  2.58 us (3%)
    pallas_call x1, Pallas kernels, shards(): pl.pallas_call(kernel, out_shape=(shape, shape), in_specs=[hbm, hbm, hbm,...  72.5 us
    unnamed x4, local copies, waits for them, and re-layouts  2.58 us

profile of v3, /device:TPU:1, one launch (start us, length us, event | category | flops | bytes accessed | tf_op | source)
XLA Modules:
  0.0 75.8 jit_solution(14658555677663734111)
XLA Ops:
  0.6 72.5 %shard_map.68 = (f32[2,3,32,512]{3,2,1,0:T(8,128)}, f32[2,3,32,512]{3,2,1,0:T(8,128)}) custom-call(f32[2,3,32,512]{3,2,1,0:T(8,128)} %b_hbm.1, f32[2,3,32,512]{3,2,1,0:T(8,128)} %prev_hbm.1, f32[3,32,512]{2,1,0:T(8,128)} %kappa_hbm.1, f32[2,3]{1,0:T(2,128)} %bitcast.1, f32[3,3]{1,0:T(4,128)} %react_s.1), custom_call_target="tpu_custom_call" | custom-call | tf_op jit(solution)/shard_map/pallas_call | solution.py:513
  73.2 0.0 copy-start
  73.2 1.8 %copy.9 = f32[2,3,32,512]{3,2,1,0:T(8,128)} copy(f32[2,3,32,512]{3,2,1,0:T(8,128)} %get-tuple-element.4) | data formatting | bytes 786432
  75.0 0.0 copy-done
  75.0 0.7 copy.10
Async XLA Ops:
  73.2 1.8 %copy-start = (f32[2,3,32,512]{3,2,1,0:T(8,128)S(1)}, f32[2,3,32,512]{3,2,1,0:T(8,128)}, u32[]{:S(2)}) copy-start(f32[2,3,32,512]{3,2,1,0:T(8,128)} %get-tuple-element.5) | copy-start | bytes 1179652

commit v4 on v3

--- a/solution.py
+++ b/solution.py
@@ -13,24 +13,21 @@
 F32 = jnp.float32
 
 
-def place_of(tile, space):
-    r, c = tile // 8, tile % 8
-    odd = space % 2
+div, rem = lax.div, lax.rem
+
+
+def place_of(r, c, odd):
     q = r + odd * (3 - 2 * r)
-    half = c // 4
-    y = (c % 4) + half * (3 - 2 * (c % 4))
-    z = q + half * (7 - 2 * q)
-    return y * 8 + z
-
-
-def tile_of(tm, space):
-    y, z = tm // 8, tm % 8
-    half = z // 4
+    half, y = div(c, 4), rem(c, 4)
+    y = y + half * (3 - 2 * y)
+    return y * 8 + q + half * (7 - 2 * q)
+
+
+def tile_of(y, z, odd):
+    half = div(z, 4)
     q = z + half * (7 - 2 * z)
     c = half * 4 + y + half * (3 - 2 * y)
-    odd = space % 2
-    r = q + odd * (3 - 2 * q)
-    return r * 8 + c
+    return (q + odd * (3 - 2 * q)) * 8 + c
 
 
 HOPS = [(dy, dz) for dz in (4, 3, 5, 2, 6, 1, 7, 0) for dy in (2, 1, 3, 0) if (dy, dz) != (0, 0)]
@@ -42,15 +39,16 @@
     out_u, out_res,
     bv, prev_v, kap, pack, msgs, held, prev_s, prev_r, ua, ub, m5, m6, back5, back6, wn,
     row_s, row_r, col_s, col_r, edge_s, edge_r, edge_n, coef, row_g, col_g,
-    in_sem, a_send, a_recv, p_send, p_recv, h_send, h_recv, r5_send, r5_recv, r6_send, r6_recv, e_send, e_recv,
+    in_sem, a_send, a_recv, p_send, p_recv, h_send, h_recv, r5_send, r5_recv, r6_send, r6_recv, e_send, e_recv, ready,
 ):
     me = lax.axis_index("tm")
     sp = lax.axis_index("space")
     spaces = lax.axis_size("space")
-    tile = tile_of(me, sp)
-    r, c = tile // 8, tile % 8
-    my, mz = me // 8, me % 8
-    peers = [((my + dy) % 4) * 8 + (mz + dz) % 8 for dy, dz in HOPS]
+    my, mz, odd_space = div(me, 8), rem(me, 8), rem(sp, 2)
+    tile = tile_of(my, mz, odd_space)
+    r, c = div(tile, 8), rem(tile, 8)
+    places = [(rem(my + dy, 4), rem(mz + dz, 8)) for dy, dz in HOPS]
+    peers = [y * 8 + z for y, z in places]
 
     load_b = pltpu.make_async_copy(b_hbm, bv, in_sem.at[0])
     load_k = pltpu.make_async_copy(kappa_hbm, kap, in_sem.at[1])
@@ -73,13 +71,11 @@
 
     @pl.when(sp > 0)
     def _():
-        for n in range(8):
-            pl.semaphore_signal(barrier, inc=1, device_id=(place_of(24 + n, sp - 1), sp - 1), device_id_type=MESH)
+        pl.semaphore_signal(barrier, inc=1, device_id=(me, sp - 1), device_id_type=MESH)
 
     @pl.when(sp < spaces - 1)
     def _():
-        for n in range(8):
-            pl.semaphore_signal(barrier, inc=1, device_id=(place_of(n, sp + 1), sp + 1), device_id_type=MESH)
+        pl.semaphore_signal(barrier, inc=1, device_id=(me, sp + 1), device_id_type=MESH)
 
     edge_up = jnp.logical_and(r == 0, sp > 0)
     edge_dn = jnp.logical_and(r == 3, sp < spaces - 1)
@@ -115,7 +111,7 @@
                 pack[rr * 8 + cp * 2, f] = jnp.where(high, swap(second), first)
                 pack[rr * 8 + cp * 2 + 1, f] = jnp.where(high, second, swap(first))
 
-    pl.semaphore_wait(barrier, TM - 1 + jnp.where(edge_up, TM, 0) + jnp.where(edge_dn, TM, 0))
+    pl.semaphore_wait(barrier, TM - 1 + jnp.where(sp > 0, 1, 0) + jnp.where(sp < spaces - 1, 1, 0))
 
     @pl.when(last)
     def _():
@@ -130,25 +126,25 @@
                     prev_s[rr * 8 + cp * 2, f] = fold_low(v)
                     prev_s[rr * 8 + cp * 2 + 1, f] = fold_high(v)
 
-        for p in peers:
+        for p, (y, z) in zip(peers, places):
             pltpu.make_async_remote_copy(
-                src_ref=prev_s.at[tile_of(p, sp)], dst_ref=prev_r, send_sem=p_send, recv_sem=p_recv,
+                src_ref=prev_s.at[tile_of(y, z, odd_space)], dst_ref=prev_r, send_sem=p_send, recv_sem=p_recv,
                 device_id=(p, sp), device_id_type=MESH).start()
         mine = pltpu.make_async_copy(prev_s.at[tile], prev_r, in_sem.at[2])
         mine.start()
         mine.wait()
 
-    for p in peers:
+    for p, (y, z) in zip(peers, places):
         pltpu.make_async_remote_copy(
-            src_ref=pack.at[tile_of(p, sp)], dst_ref=msgs.at[me], send_sem=a_send, recv_sem=a_recv,
+            src_ref=pack.at[tile_of(y, z, odd_space)], dst_ref=msgs.at[me], send_sem=a_send, recv_sem=a_recv,
             device_id=(p, sp), device_id_type=MESH).start()
     own = pltpu.make_async_copy(pack.at[tile], msgs.at[me], in_sem.at[3])
     own.start()
 
     load_k.wait()
     rows = pl.ds(pl.multiple_of(r * 8, 8), 8)
-    cols = pl.ds(pl.multiple_of((c // 2) * 128, 128), 128)
-    upper_half = (c % 2) == 1
+    cols = pl.ds(pl.multiple_of(div(c, 2) * 128, 128), 128)
+    upper_half = rem(c, 2) == 1
     keep = jnp.where(upper_half, lane, 127 - lane) >= 64
     ratio = []
     for f in range(3):
@@ -200,15 +196,15 @@
         col_g[0, f] = ends[3 * f + 1]
         col_g[1, f] = ends[3 * f + 2]
 
-    left = place_of(r * 8 + (c + 7) % 8, sp)
-    right = place_of(r * 8 + (c + 1) % 8, sp)
+    left = place_of(r, rem(c + 7, 8), odd_space)
+    right = place_of(r, rem(c + 1, 8), odd_space)
     up_in = r > 0
     dn_in = r < 3
     has_up = jnp.logical_or(up_in, sp > 0)
     has_dn = jnp.logical_or(dn_in, sp < spaces - 1)
-    up_tm = jnp.where(up_in, place_of(jnp.maximum(r - 1, 0) * 8 + c, sp), me)
+    up_tm = jnp.where(up_in, place_of(jnp.maximum(r - 1, 0), c, odd_space), me)
     up_sp = jnp.where(up_in, sp, jnp.maximum(sp - 1, 0))
-    dn_tm = jnp.where(dn_in, place_of(jnp.minimum(r + 1, 3) * 8 + c, sp), me)
+    dn_tm = jnp.where(dn_in, place_of(jnp.minimum(r + 1, 3), c, odd_space), me)
     dn_sp = jnp.where(dn_in, sp, jnp.minimum(sp + 1, spaces - 1))
 
     def row_copy(j, way):
@@ -296,7 +292,7 @@
                 for f in range(3):
                     before, lft, rgt = carry[3 * f:3 * f + 3]
                     rows = jnp.where(sub == 0, row_r[j, 1, f, pl.ds(m, 1), :], row_r[j, 0, f, pl.ds(m, 1), :])
-                    cols = jnp.where(inner == 0, pltpu.roll(col_r[j, 1, f], (128 - m) % 128, 1),
+                    cols = jnp.where(inner == 0, pltpu.roll(col_r[j, 1, f], rem(128 - m, 128), 1),
                                      pltpu.roll(col_r[j, 0, f], 63 - m, 1))
                     x = dst[m, f] - (coef[6, f] * rows + coef[7, f] * cols)
                     now = x + coef[8, f] * before
@@ -346,6 +342,18 @@
     came = carry_in(ends[0::3])
     send_halo(0, came, ends[1::3], ends[2::3])
 
+    @pl.when(sp > 0)
+    def _():
+        for n in range(8):
+            pl.semaphore_signal(
+                ready, inc=1, device_id=(place_of(3, jnp.int32(n), 1 - odd_space), sp - 1), device_id_type=MESH)
+
+    @pl.when(sp < spaces - 1)
+    def _():
+        for n in range(8):
+            pl.semaphore_signal(
+                ready, inc=1, device_id=(place_of(0, jnp.int32(n), 1 - odd_space), sp + 1), device_id_type=MESH)
+
     def sweep(j, came):
         interior(came, ua, ua)
         await_halo(j)
@@ -404,8 +412,9 @@
     own6 = send_back(m6, back6, r6_send, r6_recv, in_sem.at[1])
 
     def send_edge(way):
+        pl.semaphore_wait(ready, TM)
         for o in range(TM):
-            p = (me + o) % TM
+            p = rem(me + o, TM)
             pltpu.make_async_remote_copy(
                 src_ref=edge_s.at[p], dst_ref=edge_r.at[way, c], send_sem=e_send, recv_sem=e_recv.at[way],
                 device_id=(p, sp - 1 + 2 * way), device_id_type=MESH).start()
@@ -537,11 +546,11 @@
             dma, dma, dma, dma,
             dma((5, 4)), dma((5, 4)),
             dma, dma, dma, dma,
-            dma, dma((2,)),
+            dma, dma((2,)), pltpu.SemaphoreType.REGULAR,
         ],
         compiler_params=pltpu.CompilerParams(
-            collective_id=0, has_side_effects=True, vmem_limit_bytes=56 * 1024 * 1024),
-    )(right_side, previous, kappa, drift.T, reaction)
+            collective_id=0, has_side_effects=True, vmem_limit_bytes=40 * 1024 * 1024),
+    )(*[pltpu.with_memory_space_constraint(x, pltpu.HBM) for x in (right_side, previous, kappa, drift.T, reaction)])
 
 
 def solution(mesh):

time: 75.9 us -> 73.3 us (0.966)
  Pallas kernels: 72.5 us -> 71 us
  local copies, waits for them, and re-layouts: 2.58 us -> 1.49 us
    pallas_call x1, Pallas kernels: 72.5 us -> 71 us  [shards(): pl.pallas_call(kernel, out_shape=(shape, shape), in_specs=[hbm, hbm, hbm,...]
    unnamed x4 -> x2, local copies, waits for them, and re-layouts: 2.58 us -> 1.49 us
where the time goes in v4:
time: 73.3 us; the launch traced here: 73.2 us
  Pallas kernels  71 us (97%)
  local copies, waits for them, and re-layouts  1.49 us (2%)
    pallas_call x1, Pallas kernels, shards(): pl.pallas_call(kernel, out_shape=(shape, shape), in_specs=[hbm, hbm, hbm,...  71 us
    unnamed x2, local copies, waits for them, and re-layouts  1.49 us

profile of v4, /device:TPU:1, one launch (start us, length us, event | category | flops | bytes accessed | tf_op | source)
XLA Modules:
  0.0 73.2 jit_solution(7027770776658566922)
XLA Ops:
  0.6 71.0 %shard_map.68 = (f32[2,3,32,512]{3,2,1,0:T(8,128)S(1)}, f32[2,3,32,512]{3,2,1,0:T(8,128)S(1)}) custom-call(f32[2,3,32,512]{3,2,1,0:T(8,128)} %b_hbm.1, f32[2,3,32,512]{3,2,1,0:T(8,128)} %prev_hbm.1, f32[3,32,512]{2,1,0:T(8,128)} %kappa_hbm.1, f32[2,3]{1,0:T(2,128)} %bitcast.1, f32[3,3]{1,0:T(4,128)} %react_s.1), custom_call_target="tpu_custom_call" | custom-call | tf_op jit(solution)/shard_map/pallas_call | solution.py:522
  71.7 0.7 %copy.9 = f32[2,3,32,512]{3,2,1,0:T(8,128)} copy(f32[2,3,32,512]{3,2,1,0:T(8,128)S(1)} %get-tuple-element.4) | data formatting | bytes 786432
  72.4 0.7 %copy.10 = f32[2,3,32,512]{3,2,1,0:T(8,128)} copy(f32[2,3,32,512]{3,2,1,0:T(8,128)S(1)} %get-tuple-element.5) | data formatting | bytes 786432

commit v5 on v4

--- a/solution.py
+++ b/solution.py
@@ -89,6 +89,13 @@
     def swap(x):
         return pltpu.roll(x, 64, 1)
 
+    even_lane = rem(lane, 2) == 0
+    first_odd = jnp.where(lane > 126, 0, lane) >= 63
+    slot = jnp.where(even_lane, rem(lane, 64), rem(lane + 1, 64))
+
+    def put_columns(m, x, packed):
+        return jnp.where(slot == 2 * m, pltpu.roll(x, 2 * m, 1), packed)
+
     def fold_low(x):
         return jnp.where(high, pltpu.roll(swap(x), 4, 0), x)[0:4]
 
@@ -111,8 +118,6 @@
                 pack[rr * 8 + cp * 2, f] = jnp.where(high, swap(second), first)
                 pack[rr * 8 + cp * 2 + 1, f] = jnp.where(high, second, swap(first))
 
-    pl.semaphore_wait(barrier, TM - 1 + jnp.where(sp > 0, 1, 0) + jnp.where(sp < spaces - 1, 1, 0))
-
     @pl.when(last)
     def _():
         load_p.wait()
@@ -126,6 +131,11 @@
                     prev_s[rr * 8 + cp * 2, f] = fold_low(v)
                     prev_s[rr * 8 + cp * 2 + 1, f] = fold_high(v)
 
+
+    pl.semaphore_wait(barrier, TM - 1 + jnp.where(sp > 0, 1, 0) + jnp.where(sp < spaces - 1, 1, 0))
+
+    @pl.when(last)
+    def _():
         for p, (y, z) in zip(peers, places):
             pltpu.make_async_remote_copy(
                 src_ref=prev_s.at[tile_of(y, z, odd_space)], dst_ref=prev_r, send_sem=p_send, recv_sem=p_recv,
@@ -178,23 +188,19 @@
         carry = list(carry)
         for u in range(UNROLL):
             m = i * UNROLL + u
-            here = inner == m
             for f in range(3):
-                w, lft, rgt = carry[3 * f:3 * f + 3]
+                w, packed = carry[2 * f:2 * f + 2]
                 row_g[0, f, pl.ds(m, 1), :] = w[0:1]
                 row_g[1, f, pl.ds(m, 1), :] = w[7:8]
-                lft = jnp.where(here, pltpu.roll(w, m, 1), lft)
-                rgt = jnp.where(here, pltpu.roll(w, m + 65, 1), rgt)
-                carry[3 * f:3 * f + 3] = [w * coef[8, f], lft, rgt]
+                carry[2 * f:2 * f + 2] = [w * coef[8, f], put_columns(m, w, packed)]
         return tuple(carry)
 
     start = []
     for f in range(3):
-        start += [ratio[f], zero, zero]
+        start += [ratio[f], zero]
     ends = lax.fori_loop(0, 32 // UNROLL, power, tuple(start))
     for f in range(3):
-        col_g[0, f] = ends[3 * f + 1]
-        col_g[1, f] = ends[3 * f + 2]
+        col_g[f] = ends[2 * f + 1]
 
     left = place_of(r, rem(c + 7, 8), odd_space)
     right = place_of(r, rem(c + 1, 8), odd_space)
@@ -214,7 +220,7 @@
 
     def col_copy(j, way):
         return pltpu.make_async_remote_copy(
-            src_ref=col_s.at[j, way], dst_ref=col_r.at[j, way], send_sem=h_send.at[j, 2 + way],
+            src_ref=col_s.at[j], dst_ref=col_r.at[j, way], send_sem=h_send.at[j, 2 + way],
             recv_sem=h_recv.at[j, 2 + way], device_id=((left, right)[way], sp), device_id_type=MESH)
 
     def carry_in(ends):
@@ -227,10 +233,12 @@
             out.append(jnp.where(high, other + g32 * wrap, wrap))
         return out
 
-    def send_halo(j, came, lefts, rights):
+    def send_halo(j, came, columns):
         for f in range(3):
-            col_s[j, 0, f] = lefts[f] + col_g[0, f] * jnp.where(high, came[f][:, 64:65], came[f][:, 0:1])
-            col_s[j, 1, f] = rights[f] + col_g[1, f] * jnp.where(high, came[f][:, 127:128], came[f][:, 63:64])
+            x = came[f]
+            ahead = jnp.where(even_lane, jnp.where(high, x[:, 64:65], x[:, 0:1]),
+                              jnp.where(first_odd, x[:, 63:64], x[:, 127:128]))
+            col_s[j, f] = columns[f] + col_g[f] * ahead
         col_copy(j, 0).start()
         col_copy(j, 1).start()
         for f in range(3):
@@ -257,11 +265,10 @@
         col_copy(j, 0).wait_recv()
         col_copy(j, 1).wait_recv()
 
-    def pack_border(j, m, f, u, lft, rgt):
-        here = inner == m
+    def pack_border(j, m, f, u, packed):
         row_s[j, 0, f, pl.ds(m, 1), :] = u[0:1]
         row_s[j, 1, f, pl.ds(m, 1), :] = u[7:8]
-        return jnp.where(here, pltpu.roll(u, m, 1), lft), jnp.where(here, pltpu.roll(u, m + 65, 1), rgt)
+        return put_columns(m, u, packed)
 
     def interior(came, src, dst):
         def step(i, carry):
@@ -285,25 +292,27 @@
         lax.fori_loop(0, 32 // UNROLL, step, tuple(came))
 
     def border_scan(j, dst, halo):
+        ring = [jnp.where(even_lane, pltpu.roll(col_r[j, 1, f], 65, 1), pltpu.roll(col_r[j, 0, f], 63, 1))
+                for f in range(3)]
+
         def step(i, carry):
             carry = list(carry)
             for u in range(UNROLL):
                 m = i * UNROLL + u
                 for f in range(3):
-                    before, lft, rgt = carry[3 * f:3 * f + 3]
+                    before, packed = carry[2 * f:2 * f + 2]
                     rows = jnp.where(sub == 0, row_r[j, 1, f, pl.ds(m, 1), :], row_r[j, 0, f, pl.ds(m, 1), :])
-                    cols = jnp.where(inner == 0, pltpu.roll(col_r[j, 1, f], rem(128 - m, 128), 1),
-                                     pltpu.roll(col_r[j, 0, f], 63 - m, 1))
+                    cols = pltpu.roll(ring[f], rem(128 - 2 * m, 128), 1)
                     x = dst[m, f] - (coef[6, f] * rows + coef[7, f] * cols)
                     now = x + coef[8, f] * before
                     dst[m, f] = now
                     if halo:
-                        lft, rgt = pack_border(j + 1, m, f, now, lft, rgt)
-                    carry[3 * f:3 * f + 3] = [now, lft, rgt]
+                        packed = pack_border(j + 1, m, f, now, packed)
+                    carry[2 * f:2 * f + 2] = [now, packed]
             return tuple(carry)
 
-        ends = lax.fori_loop(0, 32 // UNROLL, step, (zero,) * 9)
-        return ends[0::3], ends[1::3], ends[2::3]
+        ends = lax.fori_loop(0, 32 // UNROLL, step, (zero,) * 6)
+        return ends[0::2], ends[1::2]
 
     own.wait()
     some = pl.ds(0, TM - 1)
@@ -322,7 +331,7 @@
         for u in range(UNROLL // 2):
             h = i * (UNROLL // 2) + u
             for f in range(3):
-                before, lft, rgt = carry[3 * f:3 * f + 3]
+                before, packed = carry[2 * f:2 * f + 2]
                 g = coef[8, f]
                 a, b = msgs[h, f], msgs[16 + h, f]
                 even = g * jnp.where(high, swap(b), a)
@@ -331,16 +340,16 @@
                 held[2 * h + 1, f] = odd
                 now = even + g * before
                 ua[2 * h, f] = now
-                lft, rgt = pack_border(0, 2 * h, f, now, lft, rgt)
+                packed = pack_border(0, 2 * h, f, now, packed)
                 now = odd + g * now
                 ua[2 * h + 1, f] = now
-                lft, rgt = pack_border(0, 2 * h + 1, f, now, lft, rgt)
-                carry[3 * f:3 * f + 3] = [now, lft, rgt]
+                packed = pack_border(0, 2 * h + 1, f, now, packed)
+                carry[2 * f:2 * f + 2] = [now, packed]
         return tuple(carry)
 
-    ends = lax.fori_loop(0, 32 // UNROLL, first, (zero,) * 9)
-    came = carry_in(ends[0::3])
-    send_halo(0, came, ends[1::3], ends[2::3])
+    ends = lax.fori_loop(0, 32 // UNROLL, first, (zero,) * 6)
+    came = carry_in(ends[0::2])
+    send_halo(0, came, ends[1::2])
 
     @pl.when(sp > 0)
     def _():
@@ -357,9 +366,9 @@
     def sweep(j, came):
         interior(came, ua, ua)
         await_halo(j)
-        ends, lefts, rights = border_scan(j, ua, True)
+        ends, columns = border_scan(j, ua, True)
         came = carry_in(ends)
-        send_halo(j + 1, came, lefts, rights)
+        send_halo(j + 1, came, columns)
         return tuple(came)
 
     came = lax.fori_loop(0, 4, sweep, tuple(came))
@@ -407,7 +416,7 @@
     lax.fori_loop(0, 32 // UNROLL, fold_even, 0)
     own5 = send_back(m5, back5, r5_send, r5_recv, in_sem.at[0])
     await_halo(4)
-    ends, _, _ = border_scan(4, ub, False)
+    ends, _ = border_scan(4, ub, False)
     lax.fori_loop(0, 32 // UNROLL, to_messages, tuple(carry_in(ends)))
     own6 = send_back(m6, back6, r6_send, r6_recv, in_sem.at[1])
 
@@ -534,14 +543,14 @@
             natural,
             pltpu.VMEM((5, 2, 3, 32, 128), F32),
             pltpu.VMEM((5, 2, 3, 32, 128), F32),
-            pltpu.VMEM((5, 2, 3, 8, 128), F32),
+            pltpu.VMEM((5, 3, 8, 128), F32),
             pltpu.VMEM((5, 2, 3, 8, 128), F32),
             pltpu.VMEM((TM, 4, 128), F32),
             pltpu.VMEM((2, 8, 4, 128), F32),
             pltpu.VMEM((2, 2, 4, 512), F32),
             pltpu.VMEM((11, 3, 8, 128), F32),
             pltpu.VMEM((2, 3, 32, 128), F32),
-            pltpu.VMEM((2, 3, 8, 128), F32),
+            pltpu.VMEM((3, 8, 128), F32),
             dma((4,)),
             dma, dma, dma, dma,
             dma((5, 4)), dma((5, 4)),

time: 73.3 us -> 71.9 us (0.981)
  Pallas kernels: 71 us -> 69.6 us
    pallas_call x1, Pallas kernels: 71 us -> 69.6 us  [shards(): pl.pallas_call(kernel, out_shape=(shape, shape), in_specs=[hbm, hbm, hbm,...]
where the time goes in v5:
time: 71.9 us; the launch traced here: 71.8 us
  Pallas kernels  69.6 us (97%)
  local copies, waits for them, and re-layouts  1.49 us (2%)
    pallas_call x1, Pallas kernels, shards(): pl.pallas_call(kernel, out_shape=(shape, shape), in_specs=[hbm, hbm, hbm,...  69.6 us
    unnamed x2, local copies, waits for them, and re-layouts  1.49 us

profile of v5, /device:TPU:1, one launch (start us, length us, event | category | flops | bytes accessed | tf_op | source)
XLA Modules:
  0.0 71.8 jit_solution(14642629423600754926)
XLA Ops:
  0.6 69.6 %shard_map.68 = (f32[2,3,32,512]{3,2,1,0:T(8,128)S(1)}, f32[2,3,32,512]{3,2,1,0:T(8,128)S(1)}) custom-call(f32[2,3,32,512]{3,2,1,0:T(8,128)} %b_hbm.1, f32[2,3,32,512]{3,2,1,0:T(8,128)} %prev_hbm.1, f32[3,32,512]{2,1,0:T(8,128)} %kappa_hbm.1, f32[2,3]{1,0:T(2,128)} %bitcast.1, f32[3,3]{1,0:T(4,128)} %react_s.1), custom_call_target="tpu_custom_call" | custom-call | tf_op jit(solution)/shard_map/pallas_call | solution.py:531
  70.3 0.7 %copy.9 = f32[2,3,32,512]{3,2,1,0:T(8,128)} copy(f32[2,3,32,512]{3,2,1,0:T(8,128)S(1)} %get-tuple-element.4) | data formatting | bytes 786432
  71.0 0.7 %copy.10 = f32[2,3,32,512]{3,2,1,0:T(8,128)} copy(f32[2,3,32,512]{3,2,1,0:T(8,128)S(1)} %get-tuple-element.5) | data formatting | bytes 786432

commit v6 on v5

--- a/solution.py
+++ b/solution.py
@@ -519,6 +519,14 @@
         pltpu.make_async_copy(edge_s, edge_s, e_send).wait()
 
 
+def write_out(u, res, out_u, out_res, sem):
+    copies = [pltpu.make_async_copy(u, out_u, sem.at[0]), pltpu.make_async_copy(res, out_res, sem.at[1])]
+    for copy in copies:
+        copy.start()
+    for copy in copies:
+        copy.wait()
+
+
 def shards(previous, right_side, kappa, drift, reaction):
     hbm = pl.BlockSpec(memory_space=pltpu.HBM)
     smem = pl.BlockSpec(memory_space=pltpu.SMEM)
@@ -528,7 +536,7 @@
     held = pltpu.VMEM((TM, 3, 8, 128), F32)
     folded = pltpu.VMEM((TM, 3, 4, 128), F32)
     natural = pltpu.VMEM((2, 3, 32, 512), F32)
-    return pl.pallas_call(
+    results = pl.pallas_call(
         kernel,
         out_shape=(shape, shape),
         in_specs=[hbm, hbm, hbm, smem, smem],
@@ -560,6 +568,13 @@
         compiler_params=pltpu.CompilerParams(
             collective_id=0, has_side_effects=True, vmem_limit_bytes=40 * 1024 * 1024),
     )(*[pltpu.with_memory_space_constraint(x, pltpu.HBM) for x in (right_side, previous, kappa, drift.T, reaction)])
+    return pl.pallas_call(
+        write_out,
+        out_shape=(shape, shape),
+        in_specs=[vmem, vmem],
+        out_specs=(hbm, hbm),
+        scratch_shapes=[dma((2,))],
+    )(*[pltpu.with_memory_space_constraint(x, pltpu.VMEM) for x in results])
 
 
 def solution(mesh):

time: 71.9 us -> 71.3 us (level)
  local copies, waits for them, and re-layouts: 1.49 us -> 0 us
  Pallas kernels: 69.6 us -> 70.5 us
    unnamed x2 -> x0, local copies, waits for them, and re-layouts: 1.49 us -> none
    pallas_call x0 -> x1, Pallas kernels: none -> 0.89 us  [shards(): pl.pallas_call(write_out, out_shape=(shape, shape), in_specs=[vmem, vmem]...]
where the time goes in v6:
time: 71.3 us; the launch traced here: 71.2 us
  Pallas kernels  70.5 us (99%)
    pallas_call x1, Pallas kernels, shards(): pl.pallas_call(kernel, out_shape=(shape, shape), in_specs=[hbm, hbm, hbm,...  69.6 us

profile of v6, /device:TPU:1, one launch (start us, length us, event | category | flops | bytes accessed | tf_op | source)
XLA Modules:
  0.0 71.2 jit_solution(15411337011984851374)
XLA Ops:
  0.6 69.6 %shard_map.68 = (f32[2,3,32,512]{3,2,1,0:T(8,128)S(1)}, f32[2,3,32,512]{3,2,1,0:T(8,128)S(1)}) custom-call(f32[2,3,32,512]{3,2,1,0:T(8,128)} %b_hbm.1, f32[2,3,32,512]{3,2,1,0:T(8,128)} %prev_hbm.1, f32[3,32,512]{2,1,0:T(8,128)} %kappa_hbm.1, f32[2,3]{1,0:T(2,128)} %bitcast.1, f32[3,3]{1,0:T(4,128)} %react_s.1), custom_call_target="tpu_custom_call" | custom-call | tf_op jit(solution)/shard_map/pallas_call | solution.py:539
  70.3 0.9 %shard_map.69 = (f32[2,3,32,512]{3,2,1,0:T(8,128)}, f32[2,3,32,512]{3,2,1,0:T(8,128)}) custom-call(f32[2,3,32,512]{3,2,1,0:T(8,128)S(1)} %get-tuple-element.4.u, f32[2,3,32,512]{3,2,1,0:T(8,128)S(1)} %get-tuple-element.5.res), custom_call_target="tpu_custom_call" | custom-call | tf_op jit(solution)/shard_map/pallas_call | solution.py:571

commit v7 on v6

--- a/solution.py
+++ b/solution.py
@@ -437,11 +437,40 @@
         send_edge(1)
 
     own5.wait()
+    pltpu.make_async_copy(m5.at[some], back5.at[some], r5_recv).wait()
+
+    first_step = jnp.where(me == 0, 1.0, 0.0)
+
+    @pl.loop(0, 4)
+    def _(rr):
+        rows = pl.ds(pl.multiple_of(rr * 8, 8), 8)
+        for cp in range(4):
+            t = rr * 8 + cp * 2
+            for f in range(3):
+                o0 = jnp.where(high, swap(unfold(back5[t + 1, f])), unfold(back5[t, f]))
+                wn[0, f, rows, cp * 128:cp * 128 + 128] = o0 * (1.0 - first_step)
+
+    pltpu.make_async_copy(pack.at[some], msgs.at[some], a_send).wait()
+
+    @pl.when(last)
+    def _():
+        pltpu.make_async_copy(prev_s.at[some], prev_s.at[some], p_send).wait()
+
+    @pl.loop(0, 5)
+    def _(j):
+        @pl.when(has_up)
+        def _():
+            row_copy(j, 0).wait_send()
+
+        @pl.when(has_dn)
+        def _():
+            row_copy(j, 1).wait_send()
+
+        col_copy(j, 0).wait_send()
+        col_copy(j, 1).wait_send()
+
     own6.wait()
-    pltpu.make_async_copy(m5.at[some], back5.at[some], r5_recv).wait()
     pltpu.make_async_copy(m6.at[some], back6.at[some], r6_recv).wait()
-
-    first_step = jnp.where(me == 0, 1.0, 0.0)
 
     @pl.loop(0, 4)
     def _(rr):
@@ -453,10 +482,9 @@
                 a6, b6 = back6[t, f], back6[t + 1, f]
                 n0 = jnp.where(high, swap(b6), a6)
                 n1 = jnp.where(high, b6, swap(a6))
-                o0 = jnp.where(high, swap(unfold(back5[t + 1, f])), unfold(back5[t, f]))
                 out_u[0, f, rows, cols] = n0
                 out_u[1, f, rows, cols] = n1
-                wn[0, f, rows, cols] = o0 * (1.0 - first_step) - n0
+                wn[0, f, rows, cols] = wn[0, f, rows, cols] - n0
                 wn[1, f, rows, cols] = -n1
 
     @pl.when(sp < spaces - 1)
@@ -493,26 +521,8 @@
                 res = res + (own + out_u[0, f])
             out_res[s, f] = res
 
-    pltpu.make_async_copy(pack.at[some], msgs.at[some], a_send).wait()
     pltpu.make_async_copy(m5.at[some], back5.at[some], r5_send).wait()
     pltpu.make_async_copy(m6.at[some], back6.at[some], r6_send).wait()
-
-    @pl.when(last)
-    def _():
-        pltpu.make_async_copy(prev_s.at[some], prev_s.at[some], p_send).wait()
-
-    @pl.loop(0, 5)
-    def _(j):
-        @pl.when(has_up)
-        def _():
-            row_copy(j, 0).wait_send()
-
-        @pl.when(has_dn)
-        def _():
-            row_copy(j, 1).wait_send()
-
-        col_copy(j, 0).wait_send()
-        col_copy(j, 1).wait_send()
 
     @pl.when(jnp.logical_or(edge_up, edge_dn))
     def _():

time: 71.3 us -> 71.3 us (level)
  no operation moved by 1% of the time
where the time goes in v7:
time: 71.3 us; the launch traced here: 71.1 us
  Pallas kernels  70.5 us (99%)
    pallas_call x1, Pallas kernels, shards(): pl.pallas_call(kernel, out_shape=(shape, shape), in_specs=[hbm, hbm, hbm,...  69.6 us

profile of v7, /device:TPU:1, one launch (start us, length us, event | category | flops | bytes accessed | tf_op | source)
XLA Modules:
  0.0 71.1 jit_solution(7239288016134925100)
XLA Ops:
  0.6 69.6 %shard_map.68 = (f32[2,3,32,512]{3,2,1,0:T(8,128)S(1)}, f32[2,3,32,512]{3,2,1,0:T(8,128)S(1)}) custom-call(f32[2,3,32,512]{3,2,1,0:T(8,128)} %b_hbm.1, f32[2,3,32,512]{3,2,1,0:T(8,128)} %prev_hbm.1, f32[3,32,512]{2,1,0:T(8,128)} %kappa_hbm.1, f32[2,3]{1,0:T(2,128)} %bitcast.1, f32[3,3]{1,0:T(4,128)} %react_s.1), custom_call_target="tpu_custom_call" | custom-call | tf_op jit(solution)/shard_map/pallas_call | solution.py:549
  70.2 0.9 %shard_map.69 = (f32[2,3,32,512]{3,2,1,0:T(8,128)}, f32[2,3,32,512]{3,2,1,0:T(8,128)}) custom-call(f32[2,3,32,512]{3,2,1,0:T(8,128)S(1)} %get-tuple-element.4.u, f32[2,3,32,512]{3,2,1,0:T(8,128)S(1)} %get-tuple-element.5.res), custom_call_target="tpu_custom_call" | custom-call | tf_op jit(solution)/shard_map/pallas_call | solution.py:581
